TPU v7x, 32 devices: a whole 2x2x4 slice. The times are simulated.
32 devices in a mesh: horiz: 8 (over z, y), lev: 4 (over x, core).
Axes of the slice: x: 2, y: 2, z: 4, core: 2. Of those that a mesh axis runs over, the one named last changes fastest.
Arguments:
- control: float32 [64, 32, 4096], P('lev', None, 'horiz'), may hold values from -6 to 6
- members: bfloat16 [64, 4, 32, 4096], P('lev', None, None, 'horiz'), may hold values from -6 to 6
- extinction: float32 [4], replicated, may hold values from 0.5 to 2
- kernels: bfloat16 [4096, 64, 128], P('horiz', 'lev'), may hold values from 0 to 1
- innovation: bfloat16 [4096, 128], P('horiz'), may hold values from -16 to 16
- obs_weight: bfloat16 [4096, 128], P('horiz'), may hold values from 0.25 to 4
- owners: int32 [4096, 1], P('horiz'), may hold values from 0 to 7; in each aligned block of 512 rows (0 to 511, 512 to 1023, ...) at most 128 rows name the same one
- pixel_columns: int32 [4096, 128], P('horiz'), may hold values from 0 to 511
- pixel_counts: int32 [4096], P('horiz'), may hold values from 1 to 128
Outputs:
- gradient: float32 [64, 32, 4096], P('lev', None, 'horiz')
Inputs may be any that keep to these rules, and one draw needn't show every extreme that they name: `owners`: among the 512 blocks of one index of horiz, no owner is named more than 128 times, and in some index's blocks one owner is named exactly 128 times.
All inputs are finite; a program needn't handle non-finite values.
Results may differ from a plain program's by a relative error of at most 0.0037.
Values may be sent and summed in bfloat16 or wider, within the bound.
A program may use at most 128 MiB of HBM per device.

v0:
```python
import math

import jax
import jax.numpy as jnp
from jax import lax
from jax.sharding import PartitionSpec as P

LEV = 64
HALF = 4


def with_halo(value, sides, width):
    for axis, dim in sides:
        devices, length = (lax.axis_size(axis), value.shape[dim])
        up = [(i, (i + 1) % devices) for i in range(devices - 1)]
        down = [(j, i) for i, j in up]
        last = lax.slice_in_dim(value, length - width, length, axis=dim)
        first = lax.slice_in_dim(value, 0, width, axis=dim)
        before = lax.ppermute(last, axis, up)
        after = lax.ppermute(first, axis, down)
        value = jnp.concatenate([before, value, after], axis=dim)
    return value


def level_matrix():
    index_levels = jnp.arange(LEV, dtype=jnp.float32)
    spread = LEV / 8.0
    distance = index_levels[:, None] - index_levels[None, :]
    matrix = jnp.exp(-distance * distance / (2.0 * spread * spread)) / (2.5066283 * spread)
    return matrix.astype(jnp.bfloat16)


def column_taps():
    offsets = jnp.arange(2 * HALF + 1, dtype=jnp.float32) - HALF
    spread = HALF / 2.0
    weights = jnp.exp(-offsets * offsets / (2.0 * spread * spread))
    return weights / jnp.sum(weights)


def smooth_columns(values):
    tap_weights = column_taps()
    span = values.shape[2]
    padded = with_halo(values, (("horiz", 2),), HALF)
    running = jnp.zeros(values.shape, jnp.float32)
    for offset in range(2 * HALF + 1):
        running = running + tap_weights[offset] * padded[:, :, offset : offset + span]
    return running


def evolve_pixels(kernel_rows, picked):
    return jnp.sum(kernel_rows.astype(jnp.float32) * picked, axis=1)


def pixel_misfit(evolved, innov_rows, weight_rows, count_rows):
    pixel_width = evolved.shape[1]
    live_pixels = jnp.arange(pixel_width, dtype=jnp.int32)[None, :] < count_rows[:, None]
    return jnp.where(
        live_pixels,
        weight_rows.astype(jnp.float32) * (evolved - innov_rows.astype(jnp.float32)),
        0.0,
    )


def column_onehot(column_block, col_count):
    return (
        jnp.arange(col_count, dtype=jnp.int32)[:, None, None] == column_block[None, :, :]
    ).astype(jnp.float32)


def body(
    control,
    members,
    extinction,
    kernels,
    innovation,
    obs_weight,
    owners,
    pixel_columns,
    pixel_counts,
):
    lev_local, mem_count, col_count = control.shape
    level_loc = level_matrix()
    first_level = lax.axis_index("lev") * lev_local
    mine_rows = lax.dynamic_slice_in_dim(level_loc, first_level, lev_local, 0)
    mine_cols = lax.dynamic_slice_in_dim(level_loc, first_level, lev_local, 1)
    scale = 1.0 / math.sqrt(mem_count)
    control_b = control.astype(jnp.bfloat16)
    section = mine_rows
    vertical = jnp.einsum(
        "ab,bmc->amc",
        section,
        lax.all_gather(control_b, "lev", axis=0, tiled=True),
        preferred_element_type=jnp.float32,
    )
    increment = smooth_columns(vertical)
    mixed = extinction[0] * members[:, 0].astype(jnp.float32)
    for species in range(1, members.shape[1]):
        mixed = mixed + extinction[species] * members[:, species].astype(jnp.float32)
    column_field = jnp.sum(mixed * increment, axis=1) * scale
    owner_ids = owners[:, 0]
    horiz_count = lax.axis_size("horiz")
    blocks_local = owner_ids.shape[0]
    pixel_width = pixel_columns.shape[1]
    capacity = max(2, 2 * (blocks_local // horiz_count))
    total_slots = horiz_count * capacity
    owner_range = jnp.arange(horiz_count, dtype=jnp.int32)
    belongs = (owner_ids[:, None] == owner_range[None, :]).astype(jnp.float32)
    block_range = jnp.arange(blocks_local, dtype=jnp.int32)
    strictly_lower = (block_range[:, None] > block_range[None, :]).astype(jnp.float32)
    earlier = jnp.dot(strictly_lower, belongs, precision=lax.Precision.HIGHEST)
    slot_index = jnp.sum(earlier * belongs, axis=1).astype(jnp.int32)
    target_slot = owner_ids * capacity + slot_index
    placement = jnp.arange(total_slots, dtype=jnp.int32)[:, None] == target_slot[None, :]
    place_half = placement.astype(jnp.bfloat16)
    kernel_buf = (
        jnp.dot(place_half, kernels.reshape(blocks_local, -1), preferred_element_type=jnp.float32)
        .astype(jnp.bfloat16)
        .reshape((total_slots,) + kernels.shape[1:])
    )
    paired = jnp.stack([innovation, obs_weight], 1).reshape(blocks_local, -1)
    value_buf = (
        jnp.dot(place_half, paired, preferred_element_type=jnp.float32)
        .astype(jnp.bfloat16)
        .reshape(total_slots, 2, pixel_width)
    )
    index_rows = jnp.concatenate([pixel_columns, pixel_counts[:, None]], 1).astype(jnp.float32)
    index_buf = jnp.dot(
        placement.astype(jnp.float32), index_rows, precision=lax.Precision.HIGHEST
    ).astype(jnp.int32)
    column_buf = index_buf[:, :pixel_width]
    count_buf = index_buf[:, pixel_width]
    kernel_in, value_in = (
        lax.all_to_all(kernel_buf, "horiz", split_axis=0, concat_axis=0, tiled=True),
        lax.all_to_all(value_buf, "horiz", split_axis=0, concat_axis=0, tiled=True),
    )
    column_in, count_in = (
        lax.all_to_all(column_buf, "horiz", split_axis=0, concat_axis=0, tiled=True),
        lax.all_to_all(count_buf, "horiz", split_axis=0, concat_axis=0, tiled=True),
    )
    slot_group = math.gcd(total_slots, 64)
    group_count = total_slots // slot_group
    kernel_groups = kernel_in.reshape(group_count, slot_group, lev_local, pixel_width)
    column_groups = column_in.reshape(group_count, slot_group, pixel_width)

    def forward_group(operands):
        kernel_block, column_block = operands
        onehot = column_onehot(column_block, col_count)
        picked = jnp.einsum("ac,cgp->gap", column_field, onehot, precision=lax.Precision.HIGHEST)
        return evolve_pixels(kernel_block, picked)

    local_sums = lax.map(forward_group, (kernel_groups, column_groups)).reshape(
        total_slots, pixel_width
    )
    evolved = lax.psum(local_sums, "lev")
    misfit = pixel_misfit(evolved, value_in[:, 0], value_in[:, 1], count_in)
    misfit_groups = misfit.reshape(group_count, slot_group, pixel_width)

    def adjoint_group(running, operands):
        kernel_block, column_block, misfit_block = operands
        onehot = column_onehot(column_block, col_count)
        contrib = kernel_block.astype(jnp.float32) * misfit_block[:, None, :]
        return (
            running + jnp.einsum("gap,cgp->ac", contrib, onehot, precision=lax.Precision.HIGHEST),
            None,
        )

    field_grad, unused = lax.scan(
        adjoint_group,
        jnp.zeros((lev_local, col_count), jnp.float32),
        (kernel_groups, column_groups, misfit_groups),
    )
    member_grad = mixed * field_grad[:, None, :] * scale
    smoothed_b = smooth_columns(member_grad).astype(jnp.bfloat16)
    section = mine_cols
    adjoint_field = jnp.einsum(
        "ba,bmc->amc",
        section,
        lax.all_gather(smoothed_b, "lev", axis=0, tiled=True),
        preferred_element_type=jnp.float32,
    )
    return control + adjoint_field


def solution(mesh):
    placed = (
        P("lev", None, "horiz"),
        P("lev", None, None, "horiz"),
        P(),
        P("horiz", "lev", None),
        P("horiz", None),
        P("horiz", None),
        P("horiz", None),
        P("horiz", None),
        P("horiz"),
    )
    return jax.shard_map(
        body, mesh=mesh, in_specs=placed, out_specs=P("lev", None, "horiz"), check_vma=False
    )
```

profile of v0, /device:TPU:13, one launch (start us, length us, event | category | flops | bytes accessed | tf_op | source)
XLA Modules:
  0.0 519.2 jit_solution(10034451160661777724)
XLA Ops:
  45.3 19.5 %all-gather.3.cloned.1.call-done = bf16[64,32,512]{2,0,1:T(8,128)(2,1)} async-done(((bf16[16,32,512]{2,0,1:T(8,128)(2,1)}), bf16[64,32,512]{2,0,1:T(8,128)(2,1)}) %all-gather.3.cloned.1.call-update) | async-done | bytes 2097168 | tf_op jit(solution)/shard_map/all_gather | solution.py:92
  76.7 56.9 %collective-permute-done.1 = f32[16,32,4]{2,0,1:T(8,128)} collective-permute-done((f32[16,32,4]{2,0,1:T(8,128)}, f32[16,32,4]{2,0,1:T(8,128)}, u32[]{:S(2)}, u32[]{:S(2)}) %collective-permute-start.1) | collective-permute-done | bytes 8224 | tf_op jit(solution)/shard_map/ppermute | solution.py:20
  133.6 13.0 %fusion.47 = (f32[16,512]{1,0:T(8,128)S(1)}, f32[16,1,32,512]{3,0,2,1:T(8,128)S(1)}) fusion(f32[16,32,512]{2,0,1:T(8,128)S(1)} %fusion.82, f32[16,32,4]{2,0,1:T(8,128)} %collective-permute-done.1, f32[16,32,4]{2,0,1:T(8,128)} %collective-permute-done, f32[]{:T(128)} %bitcast.32, f32[]{:T(128)} %bitcast.31, f32[]{:T(128)} %bitcast.30, f32[]{:T(128)} %bitcast.29, ...), kind=kLoop, calls=%fused_computation.82 | loop fusion | flops 9953280 | bytes 4243508 | tf_op jit(solution)/shard_map/reduce_sum | solution.py:99
  152.3 123.3 %while.21 = (s32[]{:T(128)}, f32[16,64,128]{2,1,0:T(8,128)}, bf16[16,64,16,128]{3,2,1,0:T(8,128)(2,1)}, s32[16,64,128]{2,1,0:T(8,128)}, f32[16,512]{1,0:T(8,128)S(1)}, /*index=5*/s32[]{:T(128)}) while((s32[]{:T(128)}, f32[16,64,128]{2,1,0:T(8,128)}, bf16[16,64,16,128]{3,2,1,0:T(8,128)(2,1)}, s32[16,64,128]{2,1,0:T(8,128)}, ...), condition=%wide.region_5.6_spmd, body=%wide.region_3.5_spmd.sunk | while | flops 809885696 | bytes 491609 | solution.py:151
  284.3 24.9 %all-reduce.2.cloned.1.call-done = f32[1024,128]{1,0:T(8,128)} async-done(((f32[1024,128]{1,0:T(8,128)}), f32[1024,128]{1,0:T(8,128)}) %all-reduce.2.cloned.1.call-update) | async-done | bytes 524304 | tf_op jit(solution)/shard_map/psum | solution.py:154
  310.6 147.6 %while.22 = (s32[]{:T(128)}, f32[16,512]{1,0:T(8,128)S(1)}, bf16[16,64,16,128]{3,2,1,0:T(8,128)(2,1)}, f32[16,64,128]{2,1,0:T(8,128)S(1)}, s32[16,64,128]{2,1,0:T(8,128)}, /*index=5*/s32[]{:T(128)}, s32[]{:T(128)}) while((s32[]{:T(128)}, f32[16,512]{1,0:T(8,128)S(1)}, bf16[16,64,16,128]{3,2,1,0:T(8,128)(2,1)}, ...), condition=%wide.region_8.9_spmd.clone, body=%wide.region_7.8_spmd.clone.sunk | while | flops 809779200 | bytes 524395 | solution.py:167
  311.4 8.4 %fusion.105 = f32[16,512]{1,0:T(8,128)S(1)} fusion(s32[64,128]{1,0:T(8,128)S(1)} %dynamic-slice_bitcast_fusion.7, f32[64,128]{1,0:T(8,128)S(1)} %dynamic-slice_bitcast_fusion.8, bf16[16,64,16,128]{3,2,1,0:T(8,128)(2,1)} %get-tuple-element.220, s32[]{:T(128)S(6)} %copy.105, f32[16,512]{1,0:T(8,128)S(1)} %get-tuple-element.212, pred[]{:T(512)S(6)} %compare.3), kind=kOutput, calls=%fused_computation.13.clone.1 | convolution fusion | flops 809779200 | bytes 393221 | tf_op jit(solution)/shard_map/while/body/eval_jaxpr/gap,cgp->ac/dot_general | solution.py:163
  320.6 8.4 %fusion.105 = f32[16,512]{1,0:T(8,128)S(1)} fusion(s32[64,128]{1,0:T(8,128)S(1)} %dynamic-slice_bitcast_fusion.7, f32[64,128]{1,0:T(8,128)S(1)} %dynamic-slice_bitcast_fusion.8, bf16[16,64,16,128]{3,2,1,0:T(8,128)(2,1)} %get-tuple-element.220, s32[]{:T(128)S(6)} %copy.105, f32[16,512]{1,0:T(8,128)S(1)} %get-tuple-element.212, pred[]{:T(512)S(6)} %compare.3), kind=kOutput, calls=%fused_computation.13.clone.1 | convolution fusion | flops 809779200 | bytes 393221 | tf_op jit(solution)/shard_map/while/body/eval_jaxpr/gap,cgp->ac/dot_general | solution.py:163
  329.9 8.4 %fusion.105 = f32[16,512]{1,0:T(8,128)S(1)} fusion(s32[64,128]{1,0:T(8,128)S(1)} %dynamic-slice_bitcast_fusion.7, f32[64,128]{1,0:T(8,128)S(1)} %dynamic-slice_bitcast_fusion.8, bf16[16,64,16,128]{3,2,1,0:T(8,128)(2,1)} %get-tuple-element.220, s32[]{:T(128)S(6)} %copy.105, f32[16,512]{1,0:T(8,128)S(1)} %get-tuple-element.212, pred[]{:T(512)S(6)} %compare.3), kind=kOutput, calls=%fused_computation.13.clone.1 | convolution fusion | flops 809779200 | bytes 393221 | tf_op jit(solution)/shard_map/while/body/eval_jaxpr/gap,cgp->ac/dot_general | solution.py:163
  339.1 8.4 %fusion.105 = f32[16,512]{1,0:T(8,128)S(1)} fusion(s32[64,128]{1,0:T(8,128)S(1)} %dynamic-slice_bitcast_fusion.7, f32[64,128]{1,0:T(8,128)S(1)} %dynamic-slice_bitcast_fusion.8, bf16[16,64,16,128]{3,2,1,0:T(8,128)(2,1)} %get-tuple-element.220, s32[]{:T(128)S(6)} %copy.105, f32[16,512]{1,0:T(8,128)S(1)} %get-tuple-element.212, pred[]{:T(512)S(6)} %compare.3), kind=kOutput, calls=%fused_computation.13.clone.1 | convolution fusion | flops 809779200 | bytes 393221 | tf_op jit(solution)/shard_map/while/body/eval_jaxpr/gap,cgp->ac/dot_general | solution.py:163
  348.3 8.4 %fusion.105 = f32[16,512]{1,0:T(8,128)S(1)} fusion(s32[64,128]{1,0:T(8,128)S(1)} %dynamic-slice_bitcast_fusion.7, f32[64,128]{1,0:T(8,128)S(1)} %dynamic-slice_bitcast_fusion.8, bf16[16,64,16,128]{3,2,1,0:T(8,128)(2,1)} %get-tuple-element.220, s32[]{:T(128)S(6)} %copy.105, f32[16,512]{1,0:T(8,128)S(1)} %get-tuple-element.212, pred[]{:T(512)S(6)} %compare.3), kind=kOutput, calls=%fused_computation.13.clone.1 | convolution fusion | flops 809779200 | bytes 393221 | tf_op jit(solution)/shard_map/while/body/eval_jaxpr/gap,cgp->ac/dot_general | solution.py:163
  357.6 8.4 %fusion.105 = f32[16,512]{1,0:T(8,128)S(1)} fusion(s32[64,128]{1,0:T(8,128)S(1)} %dynamic-slice_bitcast_fusion.7, f32[64,128]{1,0:T(8,128)S(1)} %dynamic-slice_bitcast_fusion.8, bf16[16,64,16,128]{3,2,1,0:T(8,128)(2,1)} %get-tuple-element.220, s32[]{:T(128)S(6)} %copy.105, f32[16,512]{1,0:T(8,128)S(1)} %get-tuple-element.212, pred[]{:T(512)S(6)} %compare.3), kind=kOutput, calls=%fused_computation.13.clone.1 | convolution fusion | flops 809779200 | bytes 393221 | tf_op jit(solution)/shard_map/while/body/eval_jaxpr/gap,cgp->ac/dot_general | solution.py:163
  366.8 8.4 %fusion.105 = f32[16,512]{1,0:T(8,128)S(1)} fusion(s32[64,128]{1,0:T(8,128)S(1)} %dynamic-slice_bitcast_fusion.7, f32[64,128]{1,0:T(8,128)S(1)} %dynamic-slice_bitcast_fusion.8, bf16[16,64,16,128]{3,2,1,0:T(8,128)(2,1)} %get-tuple-element.220, s32[]{:T(128)S(6)} %copy.105, f32[16,512]{1,0:T(8,128)S(1)} %get-tuple-element.212, pred[]{:T(512)S(6)} %compare.3), kind=kOutput, calls=%fused_computation.13.clone.1 | convolution fusion | flops 809779200 | bytes 393221 | tf_op jit(solution)/shard_map/while/body/eval_jaxpr/gap,cgp->ac/dot_general | solution.py:163
  376.0 8.4 %fusion.105 = f32[16,512]{1,0:T(8,128)S(1)} fusion(s32[64,128]{1,0:T(8,128)S(1)} %dynamic-slice_bitcast_fusion.7, f32[64,128]{1,0:T(8,128)S(1)} %dynamic-slice_bitcast_fusion.8, bf16[16,64,16,128]{3,2,1,0:T(8,128)(2,1)} %get-tuple-element.220, s32[]{:T(128)S(6)} %copy.105, f32[16,512]{1,0:T(8,128)S(1)} %get-tuple-element.212, pred[]{:T(512)S(6)} %compare.3), kind=kOutput, calls=%fused_computation.13.clone.1 | convolution fusion | flops 809779200 | bytes 393221 | tf_op jit(solution)/shard_map/while/body/eval_jaxpr/gap,cgp->ac/dot_general | solution.py:163
  385.2 8.4 %fusion.105 = f32[16,512]{1,0:T(8,128)S(1)} fusion(s32[64,128]{1,0:T(8,128)S(1)} %dynamic-slice_bitcast_fusion.7, f32[64,128]{1,0:T(8,128)S(1)} %dynamic-slice_bitcast_fusion.8, bf16[16,64,16,128]{3,2,1,0:T(8,128)(2,1)} %get-tuple-element.220, s32[]{:T(128)S(6)} %copy.105, f32[16,512]{1,0:T(8,128)S(1)} %get-tuple-element.212, pred[]{:T(512)S(6)} %compare.3), kind=kOutput, calls=%fused_computation.13.clone.1 | convolution fusion | flops 809779200 | bytes 393221 | tf_op jit(solution)/shard_map/while/body/eval_jaxpr/gap,cgp->ac/dot_general | solution.py:163
  394.5 8.4 %fusion.105 = f32[16,512]{1,0:T(8,128)S(1)} fusion(s32[64,128]{1,0:T(8,128)S(1)} %dynamic-slice_bitcast_fusion.7, f32[64,128]{1,0:T(8,128)S(1)} %dynamic-slice_bitcast_fusion.8, bf16[16,64,16,128]{3,2,1,0:T(8,128)(2,1)} %get-tuple-element.220, s32[]{:T(128)S(6)} %copy.105, f32[16,512]{1,0:T(8,128)S(1)} %get-tuple-element.212, pred[]{:T(512)S(6)} %compare.3), kind=kOutput, calls=%fused_computation.13.clone.1 | convolution fusion | flops 809779200 | bytes 393221 | tf_op jit(solution)/shard_map/while/body/eval_jaxpr/gap,cgp->ac/dot_general | solution.py:163
  403.7 8.4 %fusion.105 = f32[16,512]{1,0:T(8,128)S(1)} fusion(s32[64,128]{1,0:T(8,128)S(1)} %dynamic-slice_bitcast_fusion.7, f32[64,128]{1,0:T(8,128)S(1)} %dynamic-slice_bitcast_fusion.8, bf16[16,64,16,128]{3,2,1,0:T(8,128)(2,1)} %get-tuple-element.220, s32[]{:T(128)S(6)} %copy.105, f32[16,512]{1,0:T(8,128)S(1)} %get-tuple-element.212, pred[]{:T(512)S(6)} %compare.3), kind=kOutput, calls=%fused_computation.13.clone.1 | convolution fusion | flops 809779200 | bytes 393221 | tf_op jit(solution)/shard_map/while/body/eval_jaxpr/gap,cgp->ac/dot_general | solution.py:163
  412.9 8.4 %fusion.105 = f32[16,512]{1,0:T(8,128)S(1)} fusion(s32[64,128]{1,0:T(8,128)S(1)} %dynamic-slice_bitcast_fusion.7, f32[64,128]{1,0:T(8,128)S(1)} %dynamic-slice_bitcast_fusion.8, bf16[16,64,16,128]{3,2,1,0:T(8,128)(2,1)} %get-tuple-element.220, s32[]{:T(128)S(6)} %copy.105, f32[16,512]{1,0:T(8,128)S(1)} %get-tuple-element.212, pred[]{:T(512)S(6)} %compare.3), kind=kOutput, calls=%fused_computation.13.clone.1 | convolution fusion | flops 809779200 | bytes 393221 | tf_op jit(solution)/shard_map/while/body/eval_jaxpr/gap,cgp->ac/dot_general | solution.py:163
  422.1 8.4 %fusion.105 = f32[16,512]{1,0:T(8,128)S(1)} fusion(s32[64,128]{1,0:T(8,128)S(1)} %dynamic-slice_bitcast_fusion.7, f32[64,128]{1,0:T(8,128)S(1)} %dynamic-slice_bitcast_fusion.8, bf16[16,64,16,128]{3,2,1,0:T(8,128)(2,1)} %get-tuple-element.220, s32[]{:T(128)S(6)} %copy.105, f32[16,512]{1,0:T(8,128)S(1)} %get-tuple-element.212, pred[]{:T(512)S(6)} %compare.3), kind=kOutput, calls=%fused_computation.13.clone.1 | convolution fusion | flops 809779200 | bytes 393221 | tf_op jit(solution)/shard_map/while/body/eval_jaxpr/gap,cgp->ac/dot_general | solution.py:163
  431.4 8.4 %fusion.105 = f32[16,512]{1,0:T(8,128)S(1)} fusion(s32[64,128]{1,0:T(8,128)S(1)} %dynamic-slice_bitcast_fusion.7, f32[64,128]{1,0:T(8,128)S(1)} %dynamic-slice_bitcast_fusion.8, bf16[16,64,16,128]{3,2,1,0:T(8,128)(2,1)} %get-tuple-element.220, s32[]{:T(128)S(6)} %copy.105, f32[16,512]{1,0:T(8,128)S(1)} %get-tuple-element.212, pred[]{:T(512)S(6)} %compare.3), kind=kOutput, calls=%fused_computation.13.clone.1 | convolution fusion | flops 809779200 | bytes 393221 | tf_op jit(solution)/shard_map/while/body/eval_jaxpr/gap,cgp->ac/dot_general | solution.py:163
  440.6 8.4 %fusion.105 = f32[16,512]{1,0:T(8,128)S(1)} fusion(s32[64,128]{1,0:T(8,128)S(1)} %dynamic-slice_bitcast_fusion.7, f32[64,128]{1,0:T(8,128)S(1)} %dynamic-slice_bitcast_fusion.8, bf16[16,64,16,128]{3,2,1,0:T(8,128)(2,1)} %get-tuple-element.220, s32[]{:T(128)S(6)} %copy.105, f32[16,512]{1,0:T(8,128)S(1)} %get-tuple-element.212, pred[]{:T(512)S(6)} %compare.3), kind=kOutput, calls=%fused_computation.13.clone.1 | convolution fusion | flops 809779200 | bytes 393221 | tf_op jit(solution)/shard_map/while/body/eval_jaxpr/gap,cgp->ac/dot_general | solution.py:163
  449.8 8.4 %fusion.105 = f32[16,512]{1,0:T(8,128)S(1)} fusion(s32[64,128]{1,0:T(8,128)S(1)} %dynamic-slice_bitcast_fusion.7, f32[64,128]{1,0:T(8,128)S(1)} %dynamic-slice_bitcast_fusion.8, bf16[16,64,16,128]{3,2,1,0:T(8,128)(2,1)} %get-tuple-element.220, s32[]{:T(128)S(6)} %copy.105, f32[16,512]{1,0:T(8,128)S(1)} %get-tuple-element.212, pred[]{:T(512)S(6)} %compare.3), kind=kOutput, calls=%fused_computation.13.clone.1 | convolution fusion | flops 809779200 | bytes 393221 | tf_op jit(solution)/shard_map/while/body/eval_jaxpr/gap,cgp->ac/dot_general | solution.py:163
  476.2 10.4 %fusion.25 = bf16[16,32,512]{2,0,1:T(8,128)(2,1)} fusion(f32[16,32,512]{2,0,1:T(8,128)S(1)} %fusion.71, f32[16,32,4]{2,0,1:T(8,128)} %collective-permute-done.3, f32[16,32,4]{2,0,1:T(8,128)} %collective-permute-done.2, f32[16,1,32,512]{3,0,2,1:T(8,128)S(1)} %get-tuple-element.100, f32[]{:T(128)S(6)} %mul.235, f32[16,512]{1,0:T(8,128)S(1)} %get-tuple-element.60, ...), kind=kLoop, calls=%fused_computation.60 | loop fusion | flops 7077888 | bytes 2670628 | tf_op jit(solution)/shard_map/convert_element_type | solution.py:173
  486.6 22.1 %all-gather.5.cloned.1.call-done = bf16[64,32,512]{2,0,1:T(8,128)(2,1)} async-done(((bf16[16,32,512]{2,0,1:T(8,128)(2,1)}), bf16[64,32,512]{2,0,1:T(8,128)(2,1)}) %all-gather.5.cloned.1.call-update) | async-done | bytes 2097168 | tf_op jit(solution)/shard_map/all_gather | solution.py:178
  (153 shorter events, 223.3 us)
Async XLA Ops:
  6.5 11.6 %copy-start.9 = (bf16[512,16,128]{2,1,0:T(8,128)(2,1)S(1)}, bf16[512,16,128]{2,1,0:T(8,128)(2,1)}, u32[]{:S(2)}) copy-start(bf16[512,16,128]{2,1,0:T(8,128)(2,1)} %param.16) | copy-start | bytes 6291460
  11.4 1.0 copy-start.5
  12.4 17.6 %all-to-all-start.3 = ((s32[8,128,128]{1,2,0:T(8,128)}), s32[8,128,128]{1,2,0:T(8,128)S(1)}, u32[]{:S(2)}, u32[]{:S(2)}) async-start(s32[8,128,128]{1,2,0:T(8,128)} %copy_bitcast_fusion), calls=%async_computation.3 | async-start | bytes 1048576 | tf_op jit(solution)/shard_map/all_to_all | solution.py:137
  30.0 0.8 copy-start.2
  30.9 6.5 %copy-start = (f32[16,32,512]{2,1,0:T(8,128)S(1)}, f32[16,32,512]{2,1,0:T(8,128)}, u32[]{:S(2)}) copy-start(f32[16,32,512]{2,1,0:T(8,128)} %param.13) | copy-start | bytes 3145732
  30.9 8.0 %copy-start.6 = (bf16[512,128]{1,0:T(8,128)(2,1)S(1)}, bf16[512,128]{1,0:T(8,128)(2,1)}, u32[]{:S(2)}) copy-start(bf16[512,128]{1,0:T(8,128)(2,1)} %param.18) | copy-start | bytes 393220
  30.9 115.8 %all-to-all-start = ((bf16[1024,16,128]{2,1,0:T(8,128)(2,1)}), bf16[1024,16,128]{2,1,0:T(8,128)(2,1)}, u32[]{:S(2)}, u32[]{:S(2)}) async-start(bf16[1024,16,128]{2,1,0:T(8,128)(2,1)} %bitcast.110), calls=%async_computation | async-start | bytes 8388608 | tf_op jit(solution)/shard_map/all_to_all | solution.py:133
  37.3 1.6 copy-start.7
  37.3 6.6 %copy-start.1 = (bf16[16,4,32,512]{3,2,1,0:T(8,128)(2,1)S(1)}, bf16[16,4,32,512]{3,2,1,0:T(8,128)(2,1)}, u32[]{:S(2)}) copy-start(bf16[16,4,32,512]{3,2,1,0:T(8,128)(2,1)} %param.14) | copy-start | bytes 6291460
  37.3 27.5 %all-gather.3.cloned.1.call-start = ((), (), s32[]{:S(2)}) async-start(), calls=%async_computation.4 | async-start | bytes 2621440 | tf_op jit(solution)/shard_map/all_gather | solution.py:92
  45.3 28.5 %copy-start.8 = (f32[4]{0:T(128)S(1)}, f32[4]{0:T(128)}, u32[]{:S(2)}) copy-start(f32[4]{0:T(128)} %param.15) | copy-start | bytes 52
  45.3 29.2 %copy-start.4 = (bf16[1024,256]{0,1:T(8,128)(2,1)S(1)}, bf16[1024,256]{0,1:T(8,128)(2,1)}, u32[]{:S(2)}) copy-start(bf16[1024,256]{0,1:T(8,128)(2,1)} %fusion.18) | copy-start | bytes 1572868
  45.3 30.3 %copy-start.3 = (s32[8,128,128]{1,2,0:T(8,128)S(1)}, s32[8,128,128]{1,2,0:T(8,128)}, u32[]{:S(2)}) copy-start(s32[8,128,128]{1,2,0:T(8,128)} %copy-done.2) | copy-start | bytes 1572868
  67.7 65.9 %collective-permute-start.1 = (f32[16,32,4]{2,0,1:T(8,128)}, f32[16,32,4]{2,0,1:T(8,128)}, u32[]{:S(2)}, u32[]{:S(2)}) collective-permute-start(f32[16,32,4]{2,0,1:T(8,128)} %get-tuple-element.108), channel_id=1, source_target_pairs={{4,0},{8,4},{12,8},{16,12},{20,16},{24,20},{28,24},{5,1},{9,5},{13... | collective-permute-start | bytes 24584 | tf_op jit(solution)/shard_map/ppermute | solution.py:20
  69.8 63.7 %collective-permute-start = (f32[16,32,4]{2,0,1:T(8,128)S(1)}, f32[16,32,4]{2,0,1:T(8,128)}, u32[]{:S(2)}, u32[]{:S(2)}) collective-permute-start(f32[16,32,4]{2,0,1:T(8,128)S(1)} %get-tuple-element.107), channel_id=1, source_target_pairs={{0,4},{4,8},{8,12},{12,16},{16,20},{20,24},{24,28},{1,5},{5,9},{9,... | collective-permute-start | bytes 24584 | tf_op jit(solution)/shard_map/ppermute | solution.py:19
  146.6 129.0 %all-to-all-start.2 = ((bf16[1024,2,128]{2,1,0:T(2,128)(2,1)}), bf16[1024,2,128]{2,1,0:T(2,128)(2,1)S(1)}, u32[]{:S(2)}, u32[]{:S(2)}) async-start(bf16[1024,2,128]{2,1,0:T(2,128)(2,1)} %copy.58), calls=%async_computation.2 | async-start | bytes 1048576 | tf_op jit(solution)/shard_map/all_to_all | solution.py:134
  152.3 156.9 %all-reduce.2.cloned.1.call-start = ((), (), s32[]{:S(2)}) async-start(), calls=%async_computation.5 | async-start | bytes 1048576 | tf_op jit(solution)/shard_map/psum | solution.py:154
  275.6 8.7 %all-to-all-start.1 = ((s32[8,128,1]{1,2,0:T(1,128)}), s32[8,128,1]{1,2,0:T(1,128)S(1)}, u32[]{:S(2)}, u32[]{:S(2)}) async-start(s32[8,128,1]{1,2,0:T(1,128)} %slice_bitcast_fusion.1), calls=%async_computation.1 | async-start | bytes 8192 | tf_op jit(solution)/shard_map/all_to_all | solution.py:138
  281.1 227.6 %all-gather.5.cloned.1.call-start = ((), (), s32[]{:S(2)}) async-start(), calls=%async_computation.6 | async-start | bytes 2621440 | tf_op jit(solution)/shard_map/all_gather | solution.py:178
  459.2 9.3 %collective-permute-start.3 = (f32[16,32,4]{2,0,1:T(8,128)}, f32[16,32,4]{2,0,1:T(8,128)}, u32[]{:S(2)}, u32[]{:S(2)}) collective-permute-start(f32[16,32,4]{2,0,1:T(8,128)} %get-tuple-element.106), channel_id=1, source_target_pairs={{4,0},{8,4},{12,8},{16,12},{20,16},{24,20},{28,24},{5,1},{9,5},{13... | collective-permute-start | bytes 24584 | tf_op jit(solution)/shard_map/ppermute | solution.py:20
  461.4 14.8 %collective-permute-start.2 = (f32[16,32,4]{2,0,1:T(8,128)S(1)}, f32[16,32,4]{2,0,1:T(8,128)}, u32[]{:S(2)}, u32[]{:S(2)}) collective-permute-start(f32[16,32,4]{2,0,1:T(8,128)S(1)} %get-tuple-element.105), channel_id=1, source_target_pairs={{0,4},{4,8},{8,12},{12,16},{16,20},{20,24},{24,28},{1,5},{5,9},{9,... | collective-permute-start | bytes 24584 | tf_op jit(solution)/shard_map/ppermute | solution.py:19
Sparse Core Ops, SparseCore 0:
  39.7 25.0 all-gather.2
  275.7 33.4 all-reduce.1
  486.7 21.8 all-gather.4
where the time goes:
time: 525 us; the launch traced here: 519 us
  matrix products  248 us (47%)
  waiting for transfers between devices  141 us (27%)
  local copies, waits for them, and re-layouts  51.6 us (10%)
  starting transfers between devices  35.9 us (7%)
  other arithmetic  28.7 us (5%)
  between operations  13.9 us (3%)
    dot_general x16, matrix products, adjoint_group(): jnp.einsum('gap,cgp->ac', contrib, onehot, precision=lax.Precision.HIGHEST)  135 us
    dot_general x16, matrix products, forward_group(): jnp.einsum('ac,cgp->gap', column_field, onehot, precision=lax.Precision.H...  101 us
    ppermute x2, waiting for transfers between devices, with_halo(): after = lax.ppermute(first, axis, down)  59.2 us
    psum x1, waiting for transfers between devices, body(): evolved = lax.psum(local_sums, 'lev')  24.9 us
    eq x32, local copies, waits for them, and re-layouts, column_onehot(): jnp.arange(col_count, dtype=jnp.int32)[:, None, None]  24.7 us
    all_gather x1, waiting for transfers between devices, body(): lax.all_gather(smoothed_b, 'lev', axis=0, tiled=True)  22.1 us
    all_gather x1, waiting for transfers between devices, body(): lax.all_gather(control_b, 'lev', axis=0, tiled=True)  19.5 us
    reduce_sum x1, other arithmetic, body(): column_field = jnp.sum(mixed * increment, axis=1) * scale  13 us
  transfers between devices with their start and end apart: 11, of which 8 were waited for; matrix products, arithmetic and copies ran while one was open for 30% of the time, Pallas kernels for 0%

commit v1 on v0

v1 whole, which is shorter than its diff:
```python
import functools
import math

import jax
import jax.numpy as jnp
import numpy as np
from jax import lax
from jax.experimental import pallas as pl
from jax.experimental.pallas import tpu as pltpu
from jax.sharding import PartitionSpec as P

LEV = 64
HALF = 4
LANES = 128
PAIR = 16
GROUP = 8
BF = jnp.bfloat16
F32 = jnp.float32


def level_matrix():
    index_levels = np.arange(LEV, dtype=np.float32)
    spread = np.float32(LEV / 8.0)
    distance = index_levels[:, None] - index_levels[None, :]
    matrix = np.exp(-distance * distance / (2 * spread * spread)) / (np.float32(2.5066283) * spread)
    return matrix.astype(BF)


def column_taps():
    offsets = np.arange(2 * HALF + 1, dtype=np.float32) - HALF
    spread = np.float32(HALF / 2.0)
    weights = np.exp(-offsets * offsets / (2 * spread * spread))
    return weights / np.sum(weights)


def tap_matrix(width):
    rows = np.arange(width + LANES)
    place = np.where(rows < width + HALF, rows, rows - width - 2 * HALF)
    gap = place[:, None] - np.arange(width)[None, :]
    near = (np.abs(gap) <= HALF) & (rows < width + 2 * HALF)[:, None]
    dense = np.where(near, column_taps()[np.clip(gap + HALF, 0, 2 * HALF)], 0.0).astype(np.float32)
    high = dense.astype(BF)
    low = (dense - high.astype(np.float32)).astype(BF)
    return jnp.asarray(high), jnp.asarray(low)


def spread_levels(matrix):
    dense = np.kron(matrix.astype(np.float32), np.eye(PAIR, dtype=np.float32))
    return jnp.asarray(dense.astype(BF))


def with_halo(value):
    count = lax.axis_size("horiz")
    length = value.shape[-1]
    up = [(i, i + 1) for i in range(count - 1)]
    down = [(j, i) for i, j in up]
    before = lax.ppermute(value[..., length - HALF :], "horiz", up)
    after = lax.ppermute(value[..., :HALF], "horiz", down)
    edges = jnp.concatenate([after, before], axis=-1)
    pad = [(0, 0)] * (value.ndim - 1) + [(0, LANES - 2 * HALF)]
    return jnp.concatenate([value, jnp.pad(edges, pad)], axis=-1)


def dot(a, b):
    return jnp.dot(a, b, preferred_element_type=F32)


def smooth_kernel(x_ref, hi_ref, lo_ref, out_ref):
    levels, members, ext = x_ref.shape
    x = x_ref[...].reshape(levels * members, ext)
    total = dot(x, hi_ref[...]) + dot(x, lo_ref[...])
    out_ref[...] = total.astype(BF).reshape(out_ref.shape)


def field_kernel(scale, all_ref, kron_ref, mixed_ref, out_ref):
    levels, members, width = mixed_ref.shape
    total = None
    for half in range(members // PAIR):
        part = pl.ds(half * PAIR, PAIR)
        x = all_ref[:, part, :].reshape(LEV * PAIR, width)
        inc = dot(kron_ref[...], x).reshape(levels, PAIR, width)
        term = jnp.sum(mixed_ref[:, part, :].astype(F32) * inc, axis=1)
        total = term if total is None else total + term
    total = total * scale
    for tile in range(width // LANES):
        out_ref[tile] = total[:, tile * LANES : (tile + 1) * LANES]


def forward_kernel(owner_ref, field_ref, kern_ref, col_ref, out_ref):
    blocks = col_ref.shape[0]
    tiles, levels = field_ref.shape[1], field_ref.shape[2]

    def step(group, carry):
        base = pl.multiple_of(group * GROUP, GROUP)
        cols = col_ref[pl.ds(base, GROUP), :]
        rows = []
        for i in range(GROUP):
            owner = owner_ref[base + i]
            col = jnp.broadcast_to(cols[i : i + 1, :], (levels, LANES))
            low = jnp.bitwise_and(col, LANES - 1)
            high = jnp.right_shift(col, 7)
            picked = jnp.take_along_axis(field_ref[owner, 0], low, axis=1)
            for tile in range(1, tiles):
                other = jnp.take_along_axis(field_ref[owner, tile], low, axis=1)
                picked = jnp.where(high == tile, other, picked)
            prod = picked * kern_ref[base + i].astype(F32)
            rows.append(jnp.sum(prod, axis=0, keepdims=True))
        out_ref[pl.ds(base, GROUP), :] = jnp.concatenate(rows, axis=0)
        return carry

    lax.fori_loop(0, blocks // GROUP, step, 0)


def adjoint_kernel(scale, owner_ref, kern_ref, col_ref, ev_ref, inn_ref, w_ref, out_ref):
    blocks = col_ref.shape[0]
    levels = kern_ref.shape[1]
    tiles = out_ref.shape[1] // levels
    out_ref[...] = jnp.zeros_like(out_ref)
    lane_row = lax.broadcasted_iota(jnp.int32, (LANES, LANES), 0)

    def step(group, carry):
        base = pl.multiple_of(group * GROUP, GROUP)
        cols = col_ref[pl.ds(base, GROUP), :]
        low = jnp.bitwise_and(cols, LANES - 1)
        high = jnp.right_shift(cols, 7)
        misfit = w_ref[pl.ds(base, GROUP), :] * (
            ev_ref[pl.ds(base, GROUP), :] - inn_ref[pl.ds(base, GROUP), :]
        )
        misfit = misfit * scale
        parts = [jnp.where(high == tile, misfit, 0.0) for tile in range(tiles)]
        for i in range(GROUP):
            owner = owner_ref[base + i]
            kern = kern_ref[base + i].astype(F32)
            left = jnp.concatenate(
                [(kern * part[i : i + 1, :]).astype(BF) for part in parts], axis=0
            )
            hot = jnp.where(lane_row == low[i : i + 1, :], 1.0, 0.0).astype(BF)
            out_ref[owner] += lax.dot_general(
                left, hot, (((1,), (1,)), ((), ())), preferred_element_type=F32
            )
        return carry

    lax.fori_loop(0, blocks // GROUP, step, 0)


def final_kernel(mixed_ref, fg_ref, kron_ref, hi_ref, lo_ref, control_ref, out_ref):
    levels, members, width = control_ref.shape
    ext = mixed_ref.shape[2]
    fg = fg_ref[...]
    for half in range(members // PAIR):
        part = pl.ds(half * PAIR, PAIR)
        grad = mixed_ref[:, part, :].astype(F32) * fg[:, None, :]
        grad = grad.reshape(LEV * PAIR, ext)
        high = grad.astype(BF)
        low = (grad - high.astype(F32)).astype(BF)
        mixed_levels = dot(kron_ref[...], high) + dot(kron_ref[...], low)
        high = mixed_levels.astype(BF)
        low = (mixed_levels - high.astype(F32)).astype(BF)
        total = dot(high, hi_ref[...]) + dot(high, lo_ref[...]) + dot(low, hi_ref[...])
        out_ref[:, part, :] = control_ref[:, part, :] + total.reshape(levels, PAIR, width)


def greet(partners):
    barrier = pltpu.get_barrier_semaphore()
    for device in partners:
        pl.semaphore_signal(barrier, inc=1, device_id=device, device_id_type=MESH)
    pl.semaphore_wait(barrier, len(partners))


def send(src, dst, send_sem, recv_sem, device):
    copy = pltpu.make_async_remote_copy(
        src_ref=src,
        dst_ref=dst,
        send_sem=send_sem,
        recv_sem=recv_sem,
        device_id=device,
        device_id_type=MESH,
    )
    copy.start()
    return copy


def others(axis, count):
    me = lax.axis_index(axis)
    return [lax.rem(me + k, count) for k in range(1, count)]


def gather_kernel(axis, count, x_ref, out_ref, send_sem, recv_sem):
    me = lax.axis_index(axis)
    peers = others(axis, count)
    greet([{axis: peer} for peer in peers])
    copies = [
        send(x_ref, out_ref.at[me], send_sem.at[k], recv_sem.at[k], {axis: peer})
        for k, peer in enumerate(peers)
    ]
    out_ref[me] = x_ref[...]
    for copy in copies:
        copy.wait()


def level_gather_kernel(x_ref, out_ref, far_s, far_r, near_s, near_r, on_s, on_r):
    me = lax.axis_index("lev")
    near = me + 1 - 2 * lax.rem(me, 2)
    far = lax.rem(me + 2, 4)
    greet([{"lev": near}, {"lev": far}])
    chunks = far_s.shape[0]
    rows = x_ref.shape[0] // chunks
    parts = [pl.ds(c * rows, rows) for c in range(chunks)]
    away = [
        send(x_ref.at[part], out_ref.at[me, part], far_s.at[c], far_r.at[c], {"lev": far})
        for c, part in enumerate(parts)
    ]
    beside = send(x_ref, out_ref.at[me], near_s, near_r, {"lev": near})
    out_ref[me] = x_ref[...]
    onward = []
    for c, part in enumerate(parts):
        away[c].wait_recv()
        block = out_ref.at[far, part]
        onward.append(send(block, block, on_s.at[c], on_r.at[c], {"lev": near}))
    for copy in away:
        copy.wait_send()
    beside.wait()
    for copy in onward:
        copy.wait()


def total_kernel(count, x_ref, out_ref, slots, send_a, recv_a, send_b, recv_b):
    me = lax.axis_index("lev")
    peers = others("lev", count)
    greet([{"lev": peer} for peer in peers])
    rows = x_ref.shape[0] // count
    copies = [
        send(
            x_ref.at[pl.ds(pl.multiple_of(peer * rows, rows), rows)],
            slots.at[k],
            send_a.at[k],
            recv_a.at[k],
            {"lev": peer},
        )
        for k, peer in enumerate(peers)
    ]
    mine = pl.ds(pl.multiple_of(me * rows, rows), rows)
    total = x_ref[mine, :]
    for k, copy in enumerate(copies):
        copy.wait()
        total = total + slots[k]
    out_ref[mine, :] = total
    block = out_ref.at[mine]
    copies = [
        send(block, block, send_b.at[k], recv_b.at[k], {"lev": peer})
        for k, peer in enumerate(peers)
    ]
    for copy in copies:
        copy.wait()


def return_kernel(count, levs, x_ref, out_ref, slots, send_a, recv_a, send_b, recv_b):
    me, lev = lax.axis_index("horiz"), lax.axis_index("lev")
    peers = others("horiz", count)
    sides = others("lev", levs)
    greet([{"horiz": peer} for peer in peers] + [{"lev": side} for side in sides])
    copies = [
        send(x_ref.at[peer], slots.at[k], send_a.at[k], recv_a.at[k], {"horiz": peer})
        for k, peer in enumerate(peers)
    ]
    total = x_ref[me]
    for k, copy in enumerate(copies):
        copy.wait()
        total = total + slots[k]
    out_ref[lev] = total
    block = out_ref.at[lev]
    copies = [
        send(block, block, send_b.at[k], recv_b.at[k], {"lev": side})
        for k, side in enumerate(sides)
    ]
    for copy in copies:
        copy.wait()


def vmem(count):
    return [pl.BlockSpec(memory_space=pltpu.VMEM)] * count


def smem(count):
    return [pl.BlockSpec(memory_space=pltpu.SMEM)] * count


MESH = pl.DeviceIdType.MESH
PARAMS = pltpu.CompilerParams(vmem_limit_bytes=48 * 1024 * 1024)


def call(kernel, shape, dtype, scalars, *args):
    return pl.pallas_call(
        kernel,
        out_shape=jax.ShapeDtypeStruct(shape, dtype),
        in_specs=smem(scalars) + vmem(len(args) - scalars),
        out_specs=pl.BlockSpec(memory_space=pltpu.VMEM),
        compiler_params=PARAMS,
    )(*args)


def exchange(kernel, number, shape, slots, sems, x):
    scratch = [pltpu.VMEM(slots, F32)] if slots else []
    scratch += [pltpu.SemaphoreType.DMA(size) for size in sems]
    return pl.pallas_call(
        kernel,
        out_shape=jax.ShapeDtypeStruct(shape, x.dtype),
        in_specs=vmem(1),
        out_specs=pl.BlockSpec(memory_space=pltpu.VMEM),
        scratch_shapes=scratch,
        compiler_params=pltpu.CompilerParams(
            vmem_limit_bytes=32 * 1024 * 1024, collective_id=number, has_side_effects=True
        ),
    )(x)


def body(
    control,
    members,
    extinction,
    kernels,
    innovation,
    obs_weight,
    owners,
    pixel_columns,
    pixel_counts,
):
    levels, mem_count, width = control.shape
    blocks, _, pixels = kernels.shape
    horiz = lax.axis_size("horiz")
    tiles = width // LANES
    level_loc = level_matrix()
    first = lax.axis_index("lev") * levels
    kron = lax.dynamic_slice_in_dim(
        spread_levels(level_loc), first * PAIR, levels * PAIR, 0
    )
    levs = lax.axis_size("lev")
    hi, lo = tap_matrix(width)
    scale = 1.0 / math.sqrt(mem_count)
    owner_ids = owners[:, 0]

    control_ext = with_halo(control.astype(BF))
    smooth = call(smooth_kernel, (levels, mem_count, width), BF, 0, control_ext, hi, lo)
    smooth_all = exchange(
        level_gather_kernel,
        0,
        (levs,) + smooth.shape,
        None,
        [(4,), (4,), (), (), (4,), (4,)],
        smooth,
    ).reshape((levs * levels,) + smooth.shape[1:])

    mixed = extinction[0] * members[:, 0].astype(F32)
    for species in range(1, members.shape[1]):
        mixed = mixed + extinction[species] * members[:, species].astype(F32)
    mixed_ext = with_halo(mixed.astype(BF))
    mixed_all = lax.all_gather(mixed_ext, "lev", axis=0, tiled=True)


    field = call(
        functools.partial(field_kernel, scale),
        (tiles, levels, LANES),
        F32,
        0,
        smooth_all,
        kron,
        mixed,
    )
    field_all = exchange(
        functools.partial(gather_kernel, "horiz", horiz),
        1,
        (horiz,) + field.shape,
        None,
        [(horiz - 1,)] * 2,
        field,
    )
    local = call(
        forward_kernel, (blocks, pixels), F32, 1, owner_ids, field_all, kernels, pixel_columns
    )
    evolved = exchange(
        functools.partial(total_kernel, levs),
        2,
        local.shape,
        (levs - 1, blocks // levs, pixels),
        [(levs - 1,)] * 4,
        local,
    )
    live = jnp.arange(pixels, dtype=jnp.int32)[None, :] < pixel_counts[:, None]
    weight = jnp.where(live, obs_weight.astype(F32), 0.0)
    partial = call(
        functools.partial(adjoint_kernel, scale),
        (horiz, tiles * levels, LANES),
        F32,
        1,
        owner_ids,
        kernels,
        pixel_columns,
        evolved,
        innovation.astype(F32),
        weight,
    )
    partial = partial.reshape(horiz, tiles, levels, LANES).transpose(0, 2, 1, 3)
    partial = partial.reshape(horiz, levels, width)
    edge = jnp.zeros((1, levels, HALF), F32)
    after = jnp.concatenate([partial[1:, :, :HALF], edge], axis=0)
    before = jnp.concatenate([edge, partial[:-1, :, width - HALF :]], axis=0)
    blank = jnp.zeros((horiz, levels, LANES - 2 * HALF), F32)
    partial = jnp.concatenate([partial, after, before, blank], axis=2)
    fg_all = exchange(
        functools.partial(return_kernel, horiz, levs),
        3,
        (levs, levels, width + LANES),
        (horiz - 1, levels, width + LANES),
        [(horiz - 1,)] * 2 + [(levs - 1,)] * 2,
        partial,
    ).reshape(levs * levels, width + LANES)
    return call(
        final_kernel, control.shape, F32, 0, mixed_all, fg_all, kron, hi, lo, control
    )


def solution(mesh):
    placed = (
        P("lev", None, "horiz"),
        P("lev", None, None, "horiz"),
        P(),
        P("horiz", "lev", None),
        P("horiz", None),
        P("horiz", None),
        P("horiz", None),
        P("horiz", None),
        P("horiz"),
    )
    return jax.shard_map(
        body, mesh=mesh, in_specs=placed, out_specs=P("lev", None, "horiz"), check_vma=False
    )
```

time: 525 us -> 144 us (0.27)
  matrix products: 248 us -> 0 us
  waiting for transfers between devices: 141 us -> 8.55 us
  Pallas kernels: 0 us -> 94.1 us
  local copies, waits for them, and re-layouts: 51.6 us -> 7.54 us
  starting transfers between devices: 35.9 us -> 12.5 us
  other arithmetic: 28.7 us -> 6.87 us
    dot_general x38 -> x0, matrix products: 248 us -> none  [the longest x16 135 us: adjoint_group(): jnp.einsum('gap,cgp->ac', contrib, onehot, precision=lax.Precision.HIGHEST)]
    pallas_call x0 -> x9, Pallas kernels: none -> 94.1 us  [the longest x4 56.5 us: exchange(): pl.pallas_call(kernel, out_shape=jax.ShapeDtypeStruct(shape, x.dtype), in...]
    ppermute x4, waiting for transfers between devices: 66.8 us -> 8.51 us  [the longest x2 7.55 us: with_halo(): before = lax.ppermute(value[..., length - HALF:], 'horiz', up)]
    all_gather x2 -> x1, waiting for transfers between devices: 41.6 us -> 0.02 us  [body(): mixed_all = lax.all_gather(mixed_ext, 'lev', axis=0, tiled=True)]
    psum x1 -> x0, waiting for transfers between devices: 24.9 us -> none  [body(): evolved = lax.psum(local_sums, 'lev')]
    eq x32 -> x0, local copies, waits for them, and re-layouts: 24.7 us -> none  [column_onehot(): jnp.arange(col_count, dtype=jnp.int32)[:, None, None]]
    all_to_all x4 -> x0, starting transfers between devices: 23.2 us -> none  [the longest x1 6.48 us: body(): lax.all_to_all(kernel_buf, 'horiz', split_axis=0, concat_axis=0, tiled=True)]
    reduce_sum x2 -> x0, other arithmetic: 13.7 us -> none  [the longest x1 13 us: body(): column_field = jnp.sum(mixed * increment, axis=1) * scale]
  transfers between devices with their start and end apart: 11 -> 5, of which waited for: 8 -> 3; matrix products, arithmetic and copies ran while one was open for 30% -> 3% of each run, Pallas kernels for 0% -> 63%
where the time goes in v1:
time: 144 us; the launch traced here: 143 us
  Pallas kernels  94.1 us (65%)
  between operations  13.7 us (10%)
  starting transfers between devices  12.5 us (9%)
  waiting for transfers between devices  8.55 us (6%)
  local copies, waits for them, and re-layouts  7.54 us (5%)
  other arithmetic  6.87 us (5%)
    pallas_call x4, Pallas kernels, exchange(): pl.pallas_call(kernel, out_shape=jax.ShapeDtypeStruct(shape, x.dtype), in...  56.5 us
    pallas_call x5, Pallas kernels, call(): pl.pallas_call(kernel, out_shape=jax.ShapeDtypeStruct(shape, dtype), in_s...  37.6 us
    ppermute x2, starting transfers between devices, with_halo(): before = lax.ppermute(value[..., length - HALF:], 'horiz', up)  8.31 us
    ppermute x2, waiting for transfers between devices, with_halo(): before = lax.ppermute(value[..., length - HALF:], 'horiz', up)  7.55 us
    convert_element_type x1, other arithmetic, body(): mixed_ext = with_halo(mixed.astype(BF))  4.48 us
    ppermute x2, starting transfers between devices, with_halo(): after = lax.ppermute(value[..., :HALF], 'horiz', down)  4.17 us
    unnamed x26, local copies, waits for them, and re-layouts  3.68 us
  transfers between devices with their start and end apart: 5, of which 3 were waited for; matrix products, arithmetic and copies ran while one was open for 3% of the time, Pallas kernels for 63%

profile of v1, /device:TPU:13, one launch (start us, length us, event | category | flops | bytes accessed | tf_op | source)
XLA Modules:
  0.0 143.3 jit_solution(4322982070802507324)
XLA Ops:
  6.5 1.5 %fusion.13 = (f32[1]{0:T(128)}, f32[1]{0:T(128)}, f32[1]{0:T(128)}, f32[1]{0:T(128)}) fusion(f32[4]{0:T(128)} %param.14), kind=kLoop, calls=%fused_computation.27 | loop fusion | bytes 32 | tf_op jit(solution)/shard_map/slice | solution.py:353
  8.0 4.5 %fusion.9 = (bf16[16,32,512]{2,1,0:T(8,128)(2,1)S(1)}, f32[16,32,512]{2,1,0:T(8,128)S(1)}) fusion(bf16[16,4,32,512]{3,2,1,0:T(8,128)(2,1)} %param.13, f32[]{:T(128)} %bitcast.3, f32[]{:T(128)} %bitcast.2, f32[]{:T(128)} %bitcast.1, f32[]{:T(128)} %bitcast), kind=kLoop, calls=%fused_computation.23 | loop fusion | flops 3145728 | bytes 3670032 | tf_op jit(solution)/shard_map/convert_element_type | solution.py:356
  12.6 2.3 %collective-permute-start = (bf16[16,32,4]{2,1,0:T(8,128)(2,1)S(1)}, bf16[16,32,4]{2,1,0:T(8,128)(2,1)S(1)}, u32[]{:S(2)}, u32[]{:S(2)}) collective-permute-start(bf16[16,32,4]{2,1,0:T(8,128)(2,1)S(1)} %get-tuple-element.9), channel_id=1, source_target_pairs={{4,0},{8,4},{12,8},{16,12},{20,16},{24,20},{28,24},{5,1},{9,5},{13... | collective-permute-start | bytes 12296 | tf_op jit(solution)/shard_map/ppermute | solution.py:58
  14.9 4.0 %collective-permute-start.1 = (bf16[16,32,4]{2,1,0:T(8,128)(2,1)S(1)}, bf16[16,32,4]{2,1,0:T(8,128)(2,1)S(1)}, u32[]{:S(2)}, u32[]{:S(2)}) collective-permute-start(bf16[16,32,4]{2,1,0:T(8,128)(2,1)S(1)} %get-tuple-element.10), channel_id=1, source_target_pairs={{0,4},{4,8},{8,12},{12,16},{16,20},{20,24},{24,28},{1,5},{5,9},{9,... | collective-permute-start | bytes 12296 | tf_op jit(solution)/shard_map/ppermute | solution.py:57
  18.9 1.0 collective-permute-done
  19.9 3.9 %collective-permute-done.1 = bf16[16,32,4]{2,1,0:T(8,128)(2,1)S(1)} collective-permute-done((bf16[16,32,4]{2,1,0:T(8,128)(2,1)S(1)}, bf16[16,32,4]{2,1,0:T(8,128)(2,1)S(1)}, u32[]{:S(2)}, u32[]{:S(2)}) %collective-permute-start.1) | collective-permute-done | bytes 4128 | tf_op jit(solution)/shard_map/ppermute | solution.py:57
  23.9 0.9 pad_maximum_fusion
  24.9 0.8 copy-done.8
  26.5 1.9 %collective-permute-start.2 = (bf16[16,32,4]{2,1,0:T(8,128)(2,1)}, bf16[16,32,4]{2,1,0:T(8,128)(2,1)S(1)}, u32[]{:S(2)}, u32[]{:S(2)}) collective-permute-start(bf16[16,32,4]{2,1,0:T(8,128)(2,1)} %get-tuple-element.7), channel_id=1, source_target_pairs={{4,0},{8,4},{12,8},{16,12},{20,16},{24,20},{28,24},{5,1},{9,5},{13... | collective-permute-start | bytes 12296 | tf_op jit(solution)/shard_map/ppermute | solution.py:58
  28.4 4.3 %collective-permute-start.3 = (bf16[16,32,4]{2,1,0:T(8,128)(2,1)}, bf16[16,32,4]{2,1,0:T(8,128)(2,1)}, u32[]{:S(2)}, u32[]{:S(2)}) collective-permute-start(bf16[16,32,4]{2,1,0:T(8,128)(2,1)} %get-tuple-element.8), channel_id=1, source_target_pairs={{0,4},{4,8},{8,12},{12,16},{16,20},{20,24},{24,28},{1,5},{5,9},{9,... | collective-permute-start | bytes 12296 | tf_op jit(solution)/shard_map/ppermute | solution.py:57
  32.8 1.1 constant_dynamic-slice_fusion.kron_ref
  34.1 3.7 %collective-permute-done.3 = bf16[16,32,4]{2,1,0:T(8,128)(2,1)} collective-permute-done((bf16[16,32,4]{2,1,0:T(8,128)(2,1)}, bf16[16,32,4]{2,1,0:T(8,128)(2,1)}, u32[]{:S(2)}, u32[]{:S(2)}) %collective-permute-start.3) | collective-permute-done | bytes 4128 | tf_op jit(solution)/shard_map/ppermute | solution.py:57
  37.8 1.0 fusion.7
  38.9 1.1 copy-done.4
  40.0 1.0 shard_map.118.x_ref
  41.0 21.1 %shard_map.119 = bf16[4,16,32,512]{3,2,1,0:T(8,128)(2,1)S(1)} custom-call(bf16[16,32,512]{2,1,0:T(8,128)(2,1)S(1)} %shard_map.118.x_ref), custom_call_target="tpu_custom_call" | custom-call | tf_op jit(solution)/shard_map/pallas_call | solution.py:305
  62.2 0.8 shard_map.120.x_ref
  63.0 10.3 %shard_map.121.field_ref = f32[8,4,16,128]{3,2,1,0:T(8,128)S(1)} custom-call(f32[4,16,128]{2,1,0:T(8,128)S(1)} %shard_map.120.x_ref), custom_call_target="tpu_custom_call" | custom-call | tf_op jit(solution)/shard_map/pallas_call | solution.py:305
  73.2 12.2 %shard_map.122.x_ref = f32[512,128]{1,0:T(8,128)S(1)} custom-call(s32[512]{0:T(512)S(1)} %bitcast.29, f32[8,4,16,128]{3,2,1,0:T(8,128)S(1)} %shard_map.121.field_ref, bf16[512,16,128]{2,1,0:T(8,128)(2,1)S(1)} %copy-done, s32[512,128]{1,0:T(8,128)S(1)} %copy-done.6), custom_call_target="tpu_custom_call" | custom-call | tf_op jit(solution)/shard_map/pallas_call | solution.py:293
  85.4 9.8 %shard_map.123.ev_ref = f32[512,128]{1,0:T(8,128)S(1)} custom-call(f32[512,128]{1,0:T(8,128)S(1)} %shard_map.122.x_ref), custom_call_target="tpu_custom_call" | custom-call | tf_op jit(solution)/shard_map/pallas_call | solution.py:305
  95.2 19.3 %shard_map.124 = f32[8,64,128]{2,1,0:T(8,128)S(1)} custom-call(s32[512]{0:T(512)S(1)} %bitcast.30, bf16[512,16,128]{2,1,0:T(8,128)(2,1)S(1)} %copy-done, s32[512,128]{1,0:T(8,128)S(1)} %copy-done.6, f32[512,128]{1,0:T(8,128)S(1)} %shard_map.123.ev_ref, f32[512,128]{1,0:T(8,128)S(1)} %convert_element_type.37.inn_ref, f32[512,128]{1,0:T(8,128)S(1)} %convert_select_fusion.w_ref), custom_call_target="tpu_custom_call" | custom-call | tf_op jit(solution)/shard_map/pallas_call | solution.py:293
  115.0 15.3 %shard_map.125 = f32[4,16,640]{2,1,0:T(8,128)S(1)} custom-call(f32[8,16,640]{2,1,0:T(8,128)S(1)} %fusion.x_ref), custom_call_target="tpu_custom_call" | custom-call | tf_op jit(solution)/shard_map/pallas_call | solution.py:305
  130.3 1.7 %copy-done.2 = bf16[64,32,640]{2,1,0:T(8,128)(2,1)S(1)} copy-done((bf16[64,32,640]{2,1,0:T(8,128)(2,1)S(1)}, bf16[64,32,640]{2,1,0:T(8,128)(2,1)}, u32[]{:S(2)}) %copy-start.2) | copy-done | bytes 2621464
  132.1 4.3 %shard_map.126 = f32[16,32,512]{2,1,0:T(8,128)} custom-call(bf16[64,32,640]{2,1,0:T(8,128)(2,1)S(1)} %copy-done.2, f32[64,640]{1,0:T(8,128)S(1)} %bitcast.28, bf16[256,1024]{1,0:T(8,128)(2,1)S(1)} %constant_dynamic-slice_fusion.kron_ref, bf16[640,512]{1,0:T(8,128)(2,1)S(1)} %copy-done.3, bf16[640,512]{1,0:T(8,128)(2,1)S(1)} %copy-done.5, ...), custom_call_target="tpu_custom_call" | custom-call | tf_op jit(solution)/shard_map/pallas_call | solution.py:293
  (40 shorter events, 1.8 us)
Async XLA Ops:
  6.5 123.8 %all-gather.2.cloned.1.call-start = ((), (), s32[]{:S(2)}) async-start(), calls=%async_computation | async-start | bytes 3276800 | tf_op jit(solution)/shard_map/all_gather | solution.py:357
  12.5 12.3 %copy-start.1 = (f32[16,32,512]{2,1,0:T(8,128)S(1)}, f32[16,32,512]{2,1,0:T(8,128)}, u32[]{:S(2)}) copy-start(f32[16,32,512]{2,1,0:T(8,128)} %control_ref.1) | copy-start | bytes 3145732
  12.6 7.3 %collective-permute-start = (bf16[16,32,4]{2,1,0:T(8,128)(2,1)S(1)}, bf16[16,32,4]{2,1,0:T(8,128)(2,1)S(1)}, u32[]{:S(2)}, u32[]{:S(2)}) collective-permute-start(bf16[16,32,4]{2,1,0:T(8,128)(2,1)S(1)} %get-tuple-element.9), channel_id=1, source_target_pairs={{4,0},{8,4},{12,8},{16,12},{20,16},{24,20},{28,24},{5,1},{9,5},{13... | collective-permute-start | bytes 12296 | tf_op jit(solution)/shard_map/ppermute | solution.py:58
  14.9 8.9 %collective-permute-start.1 = (bf16[16,32,4]{2,1,0:T(8,128)(2,1)S(1)}, bf16[16,32,4]{2,1,0:T(8,128)(2,1)S(1)}, u32[]{:S(2)}, u32[]{:S(2)}) collective-permute-start(bf16[16,32,4]{2,1,0:T(8,128)(2,1)S(1)} %get-tuple-element.10), channel_id=1, source_target_pairs={{0,4},{4,8},{8,12},{12,16},{16,20},{20,24},{24,28},{1,5},{5,9},{9,... | collective-permute-start | bytes 12296 | tf_op jit(solution)/shard_map/ppermute | solution.py:57
  23.9 8.8 %copy-start.10 = (bf16[512,128]{1,0:T(8,128)(2,1)S(1)}, bf16[512,128]{1,0:T(8,128)(2,1)}, u32[]{:S(2)}) copy-start(bf16[512,128]{1,0:T(8,128)(2,1)} %param.17) | copy-start | bytes 393220
  23.9 8.8 %copy-start.12 = (s32[512]{0:T(512)S(1)}, s32[512]{0:T(512)}, u32[]{:S(2)}) copy-start(s32[512]{0:T(512)} %param.20) | copy-start | bytes 6148
  24.8 9.2 %copy-start.11 = (bf16[512,128]{1,0:T(8,128)(2,1)S(1)}, bf16[512,128]{1,0:T(8,128)(2,1)}, u32[]{:S(2)}) copy-start(bf16[512,128]{1,0:T(8,128)(2,1)} %param.16) | copy-start | bytes 393220
  24.9 0.8 copy-start.8
  25.7 13.2 %copy-start.3 = (bf16[640,512]{1,0:T(8,128)(2,1)S(1)}, bf16[640,512]{1,0:T(8,128)(2,1)}, u32[]{:S(2)}) copy-start(bf16[640,512]{1,0:T(8,128)(2,1)} %constant.24.clone.hi_ref) | copy-start | bytes 1966084
  26.5 7.6 %collective-permute-start.2 = (bf16[16,32,4]{2,1,0:T(8,128)(2,1)}, bf16[16,32,4]{2,1,0:T(8,128)(2,1)S(1)}, u32[]{:S(2)}, u32[]{:S(2)}) collective-permute-start(bf16[16,32,4]{2,1,0:T(8,128)(2,1)} %get-tuple-element.7), channel_id=1, source_target_pairs={{4,0},{8,4},{12,8},{16,12},{20,16},{24,20},{28,24},{5,1},{9,5},{13... | collective-permute-start | bytes 12296 | tf_op jit(solution)/shard_map/ppermute | solution.py:58
  28.4 9.4 %collective-permute-start.3 = (bf16[16,32,4]{2,1,0:T(8,128)(2,1)}, bf16[16,32,4]{2,1,0:T(8,128)(2,1)}, u32[]{:S(2)}, u32[]{:S(2)}) collective-permute-start(bf16[16,32,4]{2,1,0:T(8,128)(2,1)} %get-tuple-element.8), channel_id=1, source_target_pairs={{0,4},{4,8},{8,12},{12,16},{16,20},{20,24},{24,28},{1,5},{5,9},{9,... | collective-permute-start | bytes 12296 | tf_op jit(solution)/shard_map/ppermute | solution.py:57
  32.7 6.1 %copy-start.9 = (bf16[16,32,512]{2,1,0:T(8,128)(2,1)S(1)}, bf16[16,32,512]{2,1,0:T(8,128)(2,1)}, u32[]{:S(2)}) copy-start(bf16[16,32,512]{2,1,0:T(8,128)(2,1)} %copy-done.8) | copy-start | bytes 1572868
  38.9 1.1 copy-start.4
  62.1 11.1 %copy-start = (bf16[512,16,128]{2,1,0:T(8,128)(2,1)S(1)}, bf16[512,16,128]{2,1,0:T(8,128)(2,1)}, u32[]{:S(2)}) copy-start(bf16[512,16,128]{2,1,0:T(8,128)(2,1)} %kern_ref.3) | copy-start | bytes 6291460
  62.1 11.1 %copy-start.6 = (s32[512,128]{1,0:T(8,128)S(1)}, s32[512,128]{1,0:T(8,128)}, u32[]{:S(2)}) copy-start(s32[512,128]{1,0:T(8,128)} %col_ref.3) | copy-start | bytes 786436
  62.2 11.1 %copy-start.7 = (s32[512,1]{0,1:T(1,128)S(1)}, s32[512,1]{0,1:T(1,128)}, u32[]{:S(2)}) copy-start(s32[512,1]{0,1:T(1,128)} %param.18) | copy-start | bytes 6148
  95.2 35.1 %copy-start.5 = (bf16[640,512]{1,0:T(8,128)(2,1)S(1)}, bf16[640,512]{1,0:T(8,128)(2,1)}, u32[]{:S(2)}) copy-start(bf16[640,512]{1,0:T(8,128)(2,1)} %constant.25.clone.lo_ref) | copy-start | bytes 1966084
  130.3 1.7 %copy-start.2 = (bf16[64,32,640]{2,1,0:T(8,128)(2,1)S(1)}, bf16[64,32,640]{2,1,0:T(8,128)(2,1)}, u32[]{:S(2)}) copy-start(bf16[64,32,640]{2,1,0:T(8,128)(2,1)} %all-gather.2.cloned.1.call-done.mixed_ref) | copy-start | bytes 7864324
Sparse Core Ops, SparseCore 0:
  25.0 31.8 all-gather.1

commit v2 on v1

--- a/solution.py
+++ b/solution.py
@@ -49,27 +49,8 @@
     return jnp.asarray(dense.astype(BF))
 
 
-def with_halo(value):
-    count = lax.axis_size("horiz")
-    length = value.shape[-1]
-    up = [(i, i + 1) for i in range(count - 1)]
-    down = [(j, i) for i, j in up]
-    before = lax.ppermute(value[..., length - HALF :], "horiz", up)
-    after = lax.ppermute(value[..., :HALF], "horiz", down)
-    edges = jnp.concatenate([after, before], axis=-1)
-    pad = [(0, 0)] * (value.ndim - 1) + [(0, LANES - 2 * HALF)]
-    return jnp.concatenate([value, jnp.pad(edges, pad)], axis=-1)
-
-
 def dot(a, b):
     return jnp.dot(a, b, preferred_element_type=F32)
-
-
-def smooth_kernel(x_ref, hi_ref, lo_ref, out_ref):
-    levels, members, ext = x_ref.shape
-    x = x_ref[...].reshape(levels * members, ext)
-    total = dot(x, hi_ref[...]) + dot(x, lo_ref[...])
-    out_ref[...] = total.astype(BF).reshape(out_ref.shape)
 
 
 def field_kernel(scale, all_ref, kron_ref, mixed_ref, out_ref):
@@ -116,12 +97,13 @@
     levels = kern_ref.shape[1]
     tiles = out_ref.shape[1] // levels
     out_ref[...] = jnp.zeros_like(out_ref)
-    lane_row = lax.broadcasted_iota(jnp.int32, (LANES, LANES), 0)
+    lane_row = lax.broadcasted_iota(jnp.int32, (LANES, LANES), 0).astype(F32).astype(BF)
+    one, zero = jnp.ones((), BF), jnp.zeros((), BF)
 
     def step(group, carry):
         base = pl.multiple_of(group * GROUP, GROUP)
         cols = col_ref[pl.ds(base, GROUP), :]
-        low = jnp.bitwise_and(cols, LANES - 1)
+        low = jnp.bitwise_and(cols, LANES - 1).astype(F32)
         high = jnp.right_shift(cols, 7)
         misfit = w_ref[pl.ds(base, GROUP), :] * (
             ev_ref[pl.ds(base, GROUP), :] - inn_ref[pl.ds(base, GROUP), :]
@@ -134,7 +116,8 @@
             left = jnp.concatenate(
                 [(kern * part[i : i + 1, :]).astype(BF) for part in parts], axis=0
             )
-            hot = jnp.where(lane_row == low[i : i + 1, :], 1.0, 0.0).astype(BF)
+            row = jnp.broadcast_to(low[i : i + 1, :], (LANES, LANES)).astype(BF)
+            hot = jnp.where(lane_row == row, one, zero)
             out_ref[owner] += lax.dot_general(
                 left, hot, (((1,), (1,)), ((), ())), preferred_element_type=F32
             )
@@ -183,6 +166,70 @@
 def others(axis, count):
     me = lax.axis_index(axis)
     return [lax.rem(me + k, count) for k in range(1, count)]
+
+
+def prepare_kernel(
+    count,
+    ext_ref,
+    control_ref,
+    members_ref,
+    hi_ref,
+    lo_ref,
+    mixed_ref,
+    ext_out,
+    smooth_ref,
+    out_tiles,
+    in_tiles,
+    send_sem,
+    recv_sem,
+):
+    levels, members, width = control_ref.shape
+    me = lax.axis_index("horiz")
+    right, left = lax.rem(me + 1, count), lax.rem(me + count - 1, count)
+    greet([{"horiz": right}, {"horiz": left}])
+    lane = lax.broadcasted_iota(jnp.int32, (levels * members, LANES), 1)
+
+    def mix(tile):
+        part = pl.ds(tile * LANES, LANES)
+        total = ext_ref[0] * members_ref[:, 0, :, part].astype(F32)
+        for species in range(1, members_ref.shape[1]):
+            total = total + ext_ref[species] * members_ref[:, species, :, part].astype(F32)
+        mixed_ref[:, :, part] = total
+        ext_out[:, :, part] = total.astype(BF)
+        return total.reshape(levels * members, LANES)
+
+    def own(tile):
+        return control_ref[:, :, pl.ds(tile * LANES, LANES)].reshape(levels * members, LANES)
+
+    last = width // LANES - 1
+    first_mix, last_mix = mix(0), mix(last)
+    to_left = jnp.where(lane < HALF, own(0), pltpu.roll(first_mix, 8, 1))
+    to_right = jnp.where(lane < 8, pltpu.roll(own(last), 8, 1), pltpu.roll(last_mix, 16, 1))
+    out_tiles[0] = to_left.astype(BF)
+    out_tiles[1] = to_right.astype(BF)
+    copies = [
+        send(out_tiles.at[k], in_tiles.at[k], send_sem.at[k], recv_sem.at[k], {"horiz": peer})
+        for k, peer in enumerate((left, right))
+    ]
+    for tile in range(1, last):
+        mix(tile)
+    x = control_ref[...].astype(BF).reshape(levels * members, width)
+    total = dot(x, hi_ref[pl.ds(0, width), :]) + dot(x, lo_ref[pl.ds(0, width), :])
+    for copy in copies:
+        copy.wait()
+    after = HALF * jnp.where(me < count - 1, 1, 0)
+    before = HALF * jnp.where(me > 0, 1, 0)
+    bit = jnp.bitwise_and(lane, 7)
+    halo = jnp.where(bit < after, in_tiles[0].astype(F32), 0.0)
+    halo = jnp.where(
+        (bit >= HALF) & (bit < HALF + before), in_tiles[1].astype(F32), halo
+    )
+    shifted = jnp.where(lane < 8, pltpu.roll(halo, LANES - 8, 1), 0.0)
+    ext_out[:, :, pl.ds(width, LANES)] = shifted.astype(BF).reshape(levels, members, LANES)
+    halo = jnp.where(lane < 8, halo, 0.0).astype(BF)
+    total = total + dot(halo, hi_ref[pl.ds(width, LANES), :])
+    total = total + dot(halo, lo_ref[pl.ds(width, LANES), :])
+    smooth_ref[...] = total.astype(BF).reshape(levels, members, width)
 
 
 def gather_kernel(axis, count, x_ref, out_ref, send_sem, recv_sem):
@@ -339,8 +386,22 @@
     scale = 1.0 / math.sqrt(mem_count)
     owner_ids = owners[:, 0]
 
-    control_ext = with_halo(control.astype(BF))
-    smooth = call(smooth_kernel, (levels, mem_count, width), BF, 0, control_ext, hi, lo)
+    strip = (levels, mem_count, width)
+    edge_tiles = pltpu.VMEM((2, levels * mem_count, LANES), BF)
+    mixed, mixed_ext, smooth = pl.pallas_call(
+        functools.partial(prepare_kernel, horiz),
+        out_shape=[
+            jax.ShapeDtypeStruct(strip, F32),
+            jax.ShapeDtypeStruct((levels, mem_count, width + LANES), BF),
+            jax.ShapeDtypeStruct(strip, BF),
+        ],
+        in_specs=smem(1) + vmem(4),
+        out_specs=vmem(3),
+        scratch_shapes=[edge_tiles, edge_tiles] + [pltpu.SemaphoreType.DMA((2,))] * 2,
+        compiler_params=pltpu.CompilerParams(
+            vmem_limit_bytes=40 * 1024 * 1024, collective_id=4, has_side_effects=True
+        ),
+    )(extinction, control, members, hi, lo)
     smooth_all = exchange(
         level_gather_kernel,
         0,
@@ -350,12 +411,8 @@
         smooth,
     ).reshape((levs * levels,) + smooth.shape[1:])
 
-    mixed = extinction[0] * members[:, 0].astype(F32)
-    for species in range(1, members.shape[1]):
-        mixed = mixed + extinction[species] * members[:, species].astype(F32)
-    mixed_ext = with_halo(mixed.astype(BF))
+    smooth_all, mixed_ext = lax.optimization_barrier((smooth_all, mixed_ext))
     mixed_all = lax.all_gather(mixed_ext, "lev", axis=0, tiled=True)
-
 
     field = call(
         functools.partial(field_kernel, scale),

time: 144 us -> 124 us (0.86)
  starting transfers between devices: 12.5 us -> 0.01 us
  waiting for transfers between devices: 8.55 us -> 0.04 us
  other arithmetic: 6.87 us -> 0.24 us
  Pallas kernels: 94.1 us -> 98.1 us
  local copies, waits for them, and re-layouts: 7.54 us -> 11.2 us
    ppermute x4 -> x0, starting transfers between devices: 12.5 us -> none  [the longest x2 8.31 us: with_halo(): before = lax.ppermute(value[..., length - HALF:], 'horiz', up)]
    pallas_call x0 -> x1, Pallas kernels: none -> 9.33 us  [body(): pl.pallas_call(functools.partial(prepare_kernel, horiz), out_shape=[jax.S...]
    ppermute x4 -> x0, waiting for transfers between devices: 8.51 us -> none  [the longest x2 7.55 us: with_halo(): before = lax.ppermute(value[..., length - HALF:], 'horiz', up)]
    unnamed x26 -> x34, local copies, waits for them, and re-layouts: 3.68 us -> 9.76 us
    convert_element_type x2 -> x0, other arithmetic: 4.55 us -> none  [the longest x1 4.48 us: body(): mixed_ext = with_halo(mixed.astype(BF))]
    pallas_call x4, Pallas kernels: 56.5 us -> 52.1 us  [exchange(): pl.pallas_call(kernel, out_shape=jax.ShapeDtypeStruct(shape, x.dtype), in...]
    slice x3 -> x0, local copies, waits for them, and re-layouts: 2.35 us -> none  [the longest x1 1.47 us: body(): mixed = extinction[0] * members[:, 0].astype(F32)]
    concatenate x4 -> x0, other arithmetic: 2.08 us -> none  [the longest x2 1.13 us: with_halo(): edges = jnp.concatenate([after, before], axis=-1)]
  transfers between devices with their start and end apart: 5 -> 1, of which waited for: 3 -> 0; matrix products, arithmetic and copies ran while one was open for 3% -> 1% of each run, Pallas kernels for 63% -> 55%
where the time goes in v2:
time: 124 us; the launch traced here: 123 us
  Pallas kernels  98.1 us (79%)
  between operations  13.7 us (11%)
  local copies, waits for them, and re-layouts  11.2 us (9%)
    pallas_call x4, Pallas kernels, exchange(): pl.pallas_call(kernel, out_shape=jax.ShapeDtypeStruct(shape, x.dtype), in...  52.1 us
    pallas_call x4, Pallas kernels, call(): pl.pallas_call(kernel, out_shape=jax.ShapeDtypeStruct(shape, dtype), in_s...  36.7 us
    unnamed x34, local copies, waits for them, and re-layouts  9.76 us
    pallas_call x1, Pallas kernels, body(): pl.pallas_call(functools.partial(prepare_kernel, horiz), out_shape=[jax.S...  9.33 us
  transfers between devices with their start and end apart: 1, of which 0 were waited for; matrix products, arithmetic and copies ran while one was open for 1% of the time, Pallas kernels for 55%

profile of v2, /device:TPU:13, one launch (start us, length us, event | category | flops | bytes accessed | tf_op | source)
XLA Modules:
  0.0 123.3 jit_solution(11412465375510035557)
XLA Ops:
  6.5 1.2 copy-done.1
  7.8 1.1 copy-done.4
  8.9 1.1 copy-done.6
  9.9 1.6 %copy-done.8 = bf16[16,4,32,512]{3,2,1,0:T(8,128)(2,1)S(1)} copy-done((bf16[16,4,32,512]{3,2,1,0:T(8,128)(2,1)S(1)}, bf16[16,4,32,512]{3,2,1,0:T(8,128)(2,1)}, u32[]{:S(2)}) %copy-start.8) | copy-done | bytes 2097176
  11.5 0.7 copy-done.13
  12.2 9.3 %shard_map.118 = (f32[16,32,512]{2,1,0:T(8,128)S(1)}, bf16[16,32,640]{2,1,0:T(8,128)(2,1)}, bf16[16,32,512]{2,1,0:T(8,128)(2,1)S(1)}) custom-call(f32[4]{0:T(128)S(1)} %copy-done.13, f32[16,32,512]{2,1,0:T(8,128)S(1)} %copy-done.1, bf16[16,4,32,512]{3,2,1,0:T(8,128)(2,1)S(1)} %copy-done.8, bf16[640,512]{1,0:T(8,128)(2,1)S(1)} %copy-done.4, ...), custom_call_target="tpu_custom_call" | custom-call | tf_op jit(solution)/shard_map/pallas_call | solution.py:391
  21.5 1.0 copy-done.9
  22.5 16.6 %shard_map.119 = bf16[4,16,32,512]{3,2,1,0:T(8,128)(2,1)S(1)} custom-call(bf16[16,32,512]{2,1,0:T(8,128)(2,1)S(1)} %get-tuple-element.10.x_ref), custom_call_target="tpu_custom_call" | custom-call | tf_op jit(solution)/shard_map/pallas_call | solution.py:352
  39.1 1.1 constant_dynamic-slice_fusion.kron_ref
  40.3 1.4 %copy-done.10 = f32[16,32,512]{2,1,0:T(8,128)S(1)} copy-done((f32[16,32,512]{2,1,0:T(8,128)S(1)}, f32[16,32,512]{2,1,0:T(8,128)}, u32[]{:S(2)}) %copy-start.10) | copy-done | bytes 1048600
  41.6 0.8 shard_map.120.x_ref
  42.4 9.7 %shard_map.121.field_ref = f32[8,4,16,128]{3,2,1,0:T(8,128)S(1)} custom-call(f32[4,16,128]{2,1,0:T(8,128)S(1)} %shard_map.120.x_ref), custom_call_target="tpu_custom_call" | custom-call | tf_op jit(solution)/shard_map/pallas_call | solution.py:352
  52.2 12.2 %shard_map.122.x_ref = f32[512,128]{1,0:T(8,128)S(1)} custom-call(s32[512]{0:T(512)S(1)} %bitcast.10, f32[8,4,16,128]{3,2,1,0:T(8,128)S(1)} %shard_map.121.field_ref, bf16[512,16,128]{2,1,0:T(8,128)(2,1)S(1)} %copy-done, s32[512,128]{1,0:T(8,128)S(1)} %copy-done.11), custom_call_target="tpu_custom_call" | custom-call | tf_op jit(solution)/shard_map/pallas_call | solution.py:340
  64.4 10.7 %shard_map.123.ev_ref = f32[512,128]{1,0:T(8,128)S(1)} custom-call(f32[512,128]{1,0:T(8,128)S(1)} %shard_map.122.x_ref), custom_call_target="tpu_custom_call" | custom-call | tf_op jit(solution)/shard_map/pallas_call | solution.py:352
  75.1 0.1 convert_select_fusion.w_ref
  75.2 19.4 %shard_map.124 = f32[8,64,128]{2,1,0:T(8,128)S(1)} custom-call(s32[512]{0:T(512)S(1)} %bitcast.11, bf16[512,16,128]{2,1,0:T(8,128)(2,1)S(1)} %copy-done, s32[512,128]{1,0:T(8,128)S(1)} %copy-done.11, f32[512,128]{1,0:T(8,128)S(1)} %shard_map.123.ev_ref, f32[512,128]{1,0:T(8,128)S(1)} %convert_element_type.6.inn_ref, f32[512,128]{1,0:T(8,128)S(1)} %convert_select_fusion.w_ref), custom_call_target="tpu_custom_call" | custom-call | tf_op jit(solution)/shard_map/pallas_call | solution.py:340
  94.7 0.1 copy.16
  94.8 0.1 reshape.15
  94.9 0.1 pad.5.clone
  95.0 0.1 fusion.3
  95.1 0.1 fusion.x_ref
  95.2 15.1 %shard_map.125 = f32[4,16,640]{2,1,0:T(8,128)S(1)} custom-call(f32[8,16,640]{2,1,0:T(8,128)S(1)} %fusion.x_ref), custom_call_target="tpu_custom_call" | custom-call | tf_op jit(solution)/shard_map/pallas_call | solution.py:352
  110.4 1.7 %copy-done.3 = bf16[64,32,640]{2,1,0:T(8,128)(2,1)S(1)} copy-done((bf16[64,32,640]{2,1,0:T(8,128)(2,1)S(1)}, bf16[64,32,640]{2,1,0:T(8,128)(2,1)}, u32[]{:S(2)}) %copy-start.3) | copy-done | bytes 2621464
  112.1 4.3 %shard_map.126 = f32[16,32,512]{2,1,0:T(8,128)} custom-call(bf16[64,32,640]{2,1,0:T(8,128)(2,1)S(1)} %copy-done.3, f32[64,640]{1,0:T(8,128)S(1)} %bitcast.9, bf16[256,1024]{1,0:T(8,128)(2,1)S(1)} %constant_dynamic-slice_fusion.kron_ref, bf16[640,512]{1,0:T(8,128)(2,1)S(1)} %copy-done.5, bf16[640,512]{1,0:T(8,128)(2,1)S(1)} %copy-done.7, ...), custom_call_target="tpu_custom_call" | custom-call | tf_op jit(solution)/shard_map/pallas_call | solution.py:340
  (31 shorter events, 0.1 us)
Async XLA Ops:
  6.5 103.8 %all-gather.2.cloned.1.call-start = ((), (), s32[]{:S(2)}) async-start(), calls=%async_computation | async-start | bytes 3276800 | tf_op jit(solution)/shard_map/all_gather | solution.py:415
  6.5 1.2 copy-start.1
  7.8 1.1 copy-start.4
  8.9 1.1 copy-start.6
  9.9 1.6 %copy-start.8 = (bf16[16,4,32,512]{3,2,1,0:T(8,128)(2,1)S(1)}, bf16[16,4,32,512]{3,2,1,0:T(8,128)(2,1)}, u32[]{:S(2)}) copy-start(bf16[16,4,32,512]{3,2,1,0:T(8,128)(2,1)} %members_ref.1) | copy-start | bytes 6291460
  11.5 0.7 copy-start.13
  21.5 1.0 copy-start.9
  40.2 11.9 %copy-start = (bf16[512,16,128]{2,1,0:T(8,128)(2,1)S(1)}, bf16[512,16,128]{2,1,0:T(8,128)(2,1)}, u32[]{:S(2)}) copy-start(bf16[512,16,128]{2,1,0:T(8,128)(2,1)} %kern_ref.3) | copy-start | bytes 6291460
  40.2 1.4 %copy-start.10 = (f32[16,32,512]{2,1,0:T(8,128)S(1)}, f32[16,32,512]{2,1,0:T(8,128)}, u32[]{:S(2)}) copy-start(f32[16,32,512]{2,1,0:T(8,128)} %copy-done.9) | copy-start | bytes 3145732
  41.6 10.5 %copy-start.11 = (s32[512,128]{1,0:T(8,128)S(1)}, s32[512,128]{1,0:T(8,128)}, u32[]{:S(2)}) copy-start(s32[512,128]{1,0:T(8,128)} %col_ref.3) | copy-start | bytes 786436
  41.6 10.5 %copy-start.12 = (s32[512,1]{0,1:T(1,128)S(1)}, s32[512,1]{0,1:T(1,128)}, u32[]{:S(2)}) copy-start(s32[512,1]{0,1:T(1,128)} %param.18) | copy-start | bytes 6148
  42.4 32.6 %copy-start.14 = (bf16[512,128]{1,0:T(8,128)(2,1)S(1)}, bf16[512,128]{1,0:T(8,128)(2,1)}, u32[]{:S(2)}) copy-start(bf16[512,128]{1,0:T(8,128)(2,1)} %param.16) | copy-start | bytes 393220
  42.4 32.7 %copy-start.15 = (bf16[512,128]{1,0:T(8,128)(2,1)S(1)}, bf16[512,128]{1,0:T(8,128)(2,1)}, u32[]{:S(2)}) copy-start(bf16[512,128]{1,0:T(8,128)(2,1)} %param.17) | copy-start | bytes 393220
  42.4 32.7 %copy-start.16 = (s32[512]{0:T(512)S(1)}, s32[512]{0:T(512)}, u32[]{:S(2)}) copy-start(s32[512]{0:T(512)} %param.20) | copy-start | bytes 6148
  94.6 15.7 %copy-start.2 = (f32[16,32,512]{2,1,0:T(8,128)S(1)}, f32[16,32,512]{2,1,0:T(8,128)}, u32[]{:S(2)}) copy-start(f32[16,32,512]{2,1,0:T(8,128)} %control_ref.3) | copy-start | bytes 3145732
  94.7 15.7 %copy-start.5 = (bf16[640,512]{1,0:T(8,128)(2,1)S(1)}, bf16[640,512]{1,0:T(8,128)(2,1)}, u32[]{:S(2)}) copy-start(bf16[640,512]{1,0:T(8,128)(2,1)} %constant.22.clone.hi_ref) | copy-start | bytes 1966084
  94.7 15.7 %copy-start.7 = (bf16[640,512]{1,0:T(8,128)(2,1)S(1)}, bf16[640,512]{1,0:T(8,128)(2,1)}, u32[]{:S(2)}) copy-start(bf16[640,512]{1,0:T(8,128)(2,1)} %constant.23.clone.lo_ref) | copy-start | bytes 1966084
  110.4 1.7 %copy-start.3 = (bf16[64,32,640]{2,1,0:T(8,128)(2,1)S(1)}, bf16[64,32,640]{2,1,0:T(8,128)(2,1)}, u32[]{:S(2)}) copy-start(bf16[64,32,640]{2,1,0:T(8,128)(2,1)} %all-gather.2.cloned.1.call-done.mixed_ref) | copy-start | bytes 7864324
Sparse Core Ops, SparseCore 0:
  39.3 25.6 all-gather.1

commit v3 on v2

--- a/solution.py
+++ b/solution.py
@@ -13,7 +13,7 @@
 HALF = 4
 LANES = 128
 PAIR = 16
-GROUP = 8
+GROUP = 32
 BF = jnp.bfloat16
 F32 = jnp.float32
 
@@ -95,7 +95,7 @@
 def adjoint_kernel(scale, owner_ref, kern_ref, col_ref, ev_ref, inn_ref, w_ref, out_ref):
     blocks = col_ref.shape[0]
     levels = kern_ref.shape[1]
-    tiles = out_ref.shape[1] // levels
+    tiles = out_ref.shape[2] // levels
     out_ref[...] = jnp.zeros_like(out_ref)
     lane_row = lax.broadcasted_iota(jnp.int32, (LANES, LANES), 0).astype(F32).astype(BF)
     one, zero = jnp.ones((), BF), jnp.zeros((), BF)
@@ -113,13 +113,13 @@
         for i in range(GROUP):
             owner = owner_ref[base + i]
             kern = kern_ref[base + i].astype(F32)
-            left = jnp.concatenate(
+            rows = jnp.concatenate(
                 [(kern * part[i : i + 1, :]).astype(BF) for part in parts], axis=0
             )
             row = jnp.broadcast_to(low[i : i + 1, :], (LANES, LANES)).astype(BF)
             hot = jnp.where(lane_row == row, one, zero)
             out_ref[owner] += lax.dot_general(
-                left, hot, (((1,), (1,)), ((), ())), preferred_element_type=F32
+                hot, rows, (((1,), (1,)), ((), ())), preferred_element_type=F32
             )
         return carry
 
@@ -446,7 +446,7 @@
     weight = jnp.where(live, obs_weight.astype(F32), 0.0)
     partial = call(
         functools.partial(adjoint_kernel, scale),
-        (horiz, tiles * levels, LANES),
+        (horiz, LANES, tiles * levels),
         F32,
         1,
         owner_ids,
@@ -456,7 +456,7 @@
         innovation.astype(F32),
         weight,
     )
-    partial = partial.reshape(horiz, tiles, levels, LANES).transpose(0, 2, 1, 3)
+    partial = partial.reshape(horiz, LANES, tiles, levels).transpose(0, 3, 2, 1)
     partial = partial.reshape(horiz, levels, width)
     edge = jnp.zeros((1, levels, HALF), F32)
     after = jnp.concatenate([partial[1:, :, :HALF], edge], axis=0)

time: 124 us -> 110 us (0.89)
  Pallas kernels: 98.1 us -> 82.4 us
  local copies, waits for them, and re-layouts: 11.2 us -> 12.9 us
    pallas_call x4, Pallas kernels: 36.7 us -> 21 us  [call(): pl.pallas_call(kernel, out_shape=jax.ShapeDtypeStruct(shape, dtype), in_s...]
  transfers between devices with their start and end apart: 1 -> 1, of which waited for: 0 -> 0; matrix products, arithmetic and copies ran while one was open for 1% -> 3% of each run, Pallas kernels for 55% -> 48%
where the time goes in v3:
time: 110 us; the launch traced here: 109 us
  Pallas kernels  82.4 us (75%)
  between operations  13.7 us (12%)
  local copies, waits for them, and re-layouts  12.9 us (12%)
    pallas_call x4, Pallas kernels, exchange(): pl.pallas_call(kernel, out_shape=jax.ShapeDtypeStruct(shape, x.dtype), in...  52 us
    pallas_call x4, Pallas kernels, call(): pl.pallas_call(kernel, out_shape=jax.ShapeDtypeStruct(shape, dtype), in_s...  21 us
    unnamed x34, local copies, waits for them, and re-layouts  9.76 us
    pallas_call x1, Pallas kernels, body(): pl.pallas_call(functools.partial(prepare_kernel, horiz), out_shape=[jax.S...  9.33 us
  transfers between devices with their start and end apart: 1, of which 0 were waited for; matrix products, arithmetic and copies ran while one was open for 3% of the time, Pallas kernels for 48%

profile of v3, /device:TPU:13, one launch (start us, length us, event | category | flops | bytes accessed | tf_op | source)
XLA Modules:
  0.0 109.2 jit_solution(10686407434851649207)
XLA Ops:
  6.5 1.2 %copy-done.1 = f32[16,32,512]{2,1,0:T(8,128)S(1)} copy-done((f32[16,32,512]{2,1,0:T(8,128)S(1)}, f32[16,32,512]{2,1,0:T(8,128)}, u32[]{:S(2)}) %copy-start.1) | copy-done | bytes 1048600
  7.8 1.1 copy-done.4
  8.9 1.1 copy-done.6
  9.9 1.6 %copy-done.8 = bf16[16,4,32,512]{3,2,1,0:T(8,128)(2,1)S(1)} copy-done((bf16[16,4,32,512]{3,2,1,0:T(8,128)(2,1)S(1)}, bf16[16,4,32,512]{3,2,1,0:T(8,128)(2,1)}, u32[]{:S(2)}) %copy-start.8) | copy-done | bytes 2097176
  11.5 0.7 copy-done.13
  12.2 9.3 %shard_map.118 = (f32[16,32,512]{2,1,0:T(8,128)S(1)}, bf16[16,32,640]{2,1,0:T(8,128)(2,1)}, bf16[16,32,512]{2,1,0:T(8,128)(2,1)S(1)}) custom-call(f32[4]{0:T(128)S(1)} %copy-done.13, f32[16,32,512]{2,1,0:T(8,128)S(1)} %copy-done.1, bf16[16,4,32,512]{3,2,1,0:T(8,128)(2,1)S(1)} %copy-done.8, bf16[640,512]{1,0:T(8,128)(2,1)S(1)} %copy-done.4, ...), custom_call_target="tpu_custom_call" | custom-call | tf_op jit(solution)/shard_map/pallas_call | solution.py:391
  21.5 1.0 copy-done.9
  22.5 16.6 %shard_map.119 = bf16[4,16,32,512]{3,2,1,0:T(8,128)(2,1)S(1)} custom-call(bf16[16,32,512]{2,1,0:T(8,128)(2,1)S(1)} %get-tuple-element.10.x_ref), custom_call_target="tpu_custom_call" | custom-call | tf_op jit(solution)/shard_map/pallas_call | solution.py:352
  39.1 1.1 constant_dynamic-slice_fusion.kron_ref
  40.3 1.4 %copy-done.10 = f32[16,32,512]{2,1,0:T(8,128)S(1)} copy-done((f32[16,32,512]{2,1,0:T(8,128)S(1)}, f32[16,32,512]{2,1,0:T(8,128)}, u32[]{:S(2)}) %copy-start.10) | copy-done | bytes 1048600
  41.6 0.8 shard_map.120.x_ref
  42.4 9.7 %shard_map.121.field_ref = f32[8,4,16,128]{3,2,1,0:T(8,128)S(1)} custom-call(f32[4,16,128]{2,1,0:T(8,128)S(1)} %shard_map.120.x_ref), custom_call_target="tpu_custom_call" | custom-call | tf_op jit(solution)/shard_map/pallas_call | solution.py:352
  52.2 8.0 %shard_map.122.x_ref = f32[512,128]{1,0:T(8,128)S(1)} custom-call(s32[512]{0:T(512)S(1)} %bitcast.12, f32[8,4,16,128]{3,2,1,0:T(8,128)S(1)} %shard_map.121.field_ref, bf16[512,16,128]{2,1,0:T(8,128)(2,1)S(1)} %copy-done, s32[512,128]{1,0:T(8,128)S(1)} %copy-done.11), custom_call_target="tpu_custom_call" | custom-call | tf_op jit(solution)/shard_map/pallas_call | solution.py:340
  60.2 10.7 %shard_map.123.ev_ref = f32[512,128]{1,0:T(8,128)S(1)} custom-call(f32[512,128]{1,0:T(8,128)S(1)} %shard_map.122.x_ref), custom_call_target="tpu_custom_call" | custom-call | tf_op jit(solution)/shard_map/pallas_call | solution.py:352
  70.9 0.1 convert_select_fusion.w_ref
  71.1 7.9 %shard_map.124 = f32[8,128,64]{2,1,0:T(8,128)S(1)} custom-call(s32[512]{0:T(512)S(1)} %bitcast.13, bf16[512,16,128]{2,1,0:T(8,128)(2,1)S(1)} %copy-done, s32[512,128]{1,0:T(8,128)S(1)} %copy-done.11, f32[512,128]{1,0:T(8,128)S(1)} %shard_map.123.ev_ref, f32[512,128]{1,0:T(8,128)S(1)} %convert_element_type.6.inn_ref, f32[512,128]{1,0:T(8,128)S(1)} %convert_select_fusion.w_ref), custom_call_target="tpu_custom_call" | custom-call | tf_op jit(solution)/shard_map/pallas_call | solution.py:340
  79.0 0.9 copy.16
  79.9 1.0 copy.20
  80.8 0.1 pad.5.clone
  80.9 0.1 fusion.3
  81.0 0.1 fusion.x_ref
  81.1 15.1 %shard_map.125 = f32[4,16,640]{2,1,0:T(8,128)S(1)} custom-call(f32[8,16,640]{2,1,0:T(8,128)S(1)} %fusion.x_ref), custom_call_target="tpu_custom_call" | custom-call | tf_op jit(solution)/shard_map/pallas_call | solution.py:352
  96.2 1.7 %copy-done.3 = bf16[64,32,640]{2,1,0:T(8,128)(2,1)S(1)} copy-done((bf16[64,32,640]{2,1,0:T(8,128)(2,1)S(1)}, bf16[64,32,640]{2,1,0:T(8,128)(2,1)}, u32[]{:S(2)}) %copy-start.3) | copy-done | bytes 2621464
  98.0 4.3 %shard_map.126 = f32[16,32,512]{2,1,0:T(8,128)} custom-call(bf16[64,32,640]{2,1,0:T(8,128)(2,1)S(1)} %copy-done.3, f32[64,640]{1,0:T(8,128)S(1)} %bitcast.11, bf16[256,1024]{1,0:T(8,128)(2,1)S(1)} %constant_dynamic-slice_fusion.kron_ref, bf16[640,512]{1,0:T(8,128)(2,1)S(1)} %copy-done.5, bf16[640,512]{1,0:T(8,128)(2,1)S(1)} %copy-done.7, ...), custom_call_target="tpu_custom_call" | custom-call | tf_op jit(solution)/shard_map/pallas_call | solution.py:340
  (31 shorter events, 0.1 us)
Async XLA Ops:
  6.5 89.7 %all-gather.2.cloned.1.call-start = ((), (), s32[]{:S(2)}) async-start(), calls=%async_computation | async-start | bytes 3276800 | tf_op jit(solution)/shard_map/all_gather | solution.py:415
  6.5 1.2 %copy-start.1 = (f32[16,32,512]{2,1,0:T(8,128)S(1)}, f32[16,32,512]{2,1,0:T(8,128)}, u32[]{:S(2)}) copy-start(f32[16,32,512]{2,1,0:T(8,128)} %control_ref.3) | copy-start | bytes 3145732
  7.8 1.1 copy-start.4
  8.9 1.1 copy-start.6
  9.9 1.6 %copy-start.8 = (bf16[16,4,32,512]{3,2,1,0:T(8,128)(2,1)S(1)}, bf16[16,4,32,512]{3,2,1,0:T(8,128)(2,1)}, u32[]{:S(2)}) copy-start(bf16[16,4,32,512]{3,2,1,0:T(8,128)(2,1)} %members_ref.1) | copy-start | bytes 6291460
  11.5 0.7 copy-start.13
  21.5 1.0 copy-start.9
  40.2 11.9 %copy-start = (bf16[512,16,128]{2,1,0:T(8,128)(2,1)S(1)}, bf16[512,16,128]{2,1,0:T(8,128)(2,1)}, u32[]{:S(2)}) copy-start(bf16[512,16,128]{2,1,0:T(8,128)(2,1)} %kern_ref.3) | copy-start | bytes 6291460
  40.2 1.4 %copy-start.10 = (f32[16,32,512]{2,1,0:T(8,128)S(1)}, f32[16,32,512]{2,1,0:T(8,128)}, u32[]{:S(2)}) copy-start(f32[16,32,512]{2,1,0:T(8,128)} %copy-done.9) | copy-start | bytes 3145732
  41.6 10.5 %copy-start.11 = (s32[512,128]{1,0:T(8,128)S(1)}, s32[512,128]{1,0:T(8,128)}, u32[]{:S(2)}) copy-start(s32[512,128]{1,0:T(8,128)} %col_ref.3) | copy-start | bytes 786436
  41.6 10.5 %copy-start.12 = (s32[512,1]{0,1:T(1,128)S(1)}, s32[512,1]{0,1:T(1,128)}, u32[]{:S(2)}) copy-start(s32[512,1]{0,1:T(1,128)} %param.18) | copy-start | bytes 6148
  42.4 28.5 %copy-start.14 = (bf16[512,128]{1,0:T(8,128)(2,1)S(1)}, bf16[512,128]{1,0:T(8,128)(2,1)}, u32[]{:S(2)}) copy-start(bf16[512,128]{1,0:T(8,128)(2,1)} %param.16) | copy-start | bytes 393220
  42.4 28.5 %copy-start.15 = (bf16[512,128]{1,0:T(8,128)(2,1)S(1)}, bf16[512,128]{1,0:T(8,128)(2,1)}, u32[]{:S(2)}) copy-start(bf16[512,128]{1,0:T(8,128)(2,1)} %param.17) | copy-start | bytes 393220
  42.4 28.5 %copy-start.16 = (s32[512]{0:T(512)S(1)}, s32[512]{0:T(512)}, u32[]{:S(2)}) copy-start(s32[512]{0:T(512)} %param.20) | copy-start | bytes 6148
  78.9 17.3 %copy-start.2 = (f32[16,32,512]{2,1,0:T(8,128)S(1)}, f32[16,32,512]{2,1,0:T(8,128)}, u32[]{:S(2)}) copy-start(f32[16,32,512]{2,1,0:T(8,128)} %control_ref.3) | copy-start | bytes 3145732
  78.9 17.3 %copy-start.5 = (bf16[640,512]{1,0:T(8,128)(2,1)S(1)}, bf16[640,512]{1,0:T(8,128)(2,1)}, u32[]{:S(2)}) copy-start(bf16[640,512]{1,0:T(8,128)(2,1)} %constant.22.clone.hi_ref) | copy-start | bytes 1966084
  79.0 17.3 %copy-start.7 = (bf16[640,512]{1,0:T(8,128)(2,1)S(1)}, bf16[640,512]{1,0:T(8,128)(2,1)}, u32[]{:S(2)}) copy-start(bf16[640,512]{1,0:T(8,128)(2,1)} %constant.23.clone.lo_ref) | copy-start | bytes 1966084
  96.2 1.7 %copy-start.3 = (bf16[64,32,640]{2,1,0:T(8,128)(2,1)S(1)}, bf16[64,32,640]{2,1,0:T(8,128)(2,1)}, u32[]{:S(2)}) copy-start(bf16[64,32,640]{2,1,0:T(8,128)(2,1)} %all-gather.2.cloned.1.call-done.mixed_ref) | copy-start | bytes 7864324
Sparse Core Ops, SparseCore 0:
  39.3 25.6 all-gather.1

commit v4 on v3

--- a/solution.py
+++ b/solution.py
@@ -13,7 +13,7 @@
 HALF = 4
 LANES = 128
 PAIR = 16
-GROUP = 32
+GROUP = 64
 BF = jnp.bfloat16
 F32 = jnp.float32
 
@@ -407,7 +407,7 @@
         0,
         (levs,) + smooth.shape,
         None,
-        [(4,), (4,), (), (), (4,), (4,)],
+        [(8,), (8,), (), (), (8,), (8,)],
         smooth,
     ).reshape((levs * levels,) + smooth.shape[1:])
 

time: 110 us -> 108 us (0.982)
  Pallas kernels: 82.4 us -> 80.4 us
    pallas_call x4, Pallas kernels: 21 us -> 19 us  [call(): pl.pallas_call(kernel, out_shape=jax.ShapeDtypeStruct(shape, dtype), in_s...]
  transfers between devices with their start and end apart: 1 -> 1, of which waited for: 0 -> 0; matrix products, arithmetic and copies ran while one was open for 3% -> 3% of each run, Pallas kernels for 48% -> 47%
where the time goes in v4:
time: 108 us; the launch traced here: 107 us
  Pallas kernels  80.4 us (74%)
  between operations  13.7 us (13%)
  local copies, waits for them, and re-layouts  12.9 us (12%)
    pallas_call x4, Pallas kernels, exchange(): pl.pallas_call(kernel, out_shape=jax.ShapeDtypeStruct(shape, x.dtype), in...  52.1 us
    pallas_call x4, Pallas kernels, call(): pl.pallas_call(kernel, out_shape=jax.ShapeDtypeStruct(shape, dtype), in_s...  19 us
    unnamed x34, local copies, waits for them, and re-layouts  9.76 us
    pallas_call x1, Pallas kernels, body(): pl.pallas_call(functools.partial(prepare_kernel, horiz), out_shape=[jax.S...  9.33 us
  transfers between devices with their start and end apart: 1, of which 0 were waited for; matrix products, arithmetic and copies ran while one was open for 3% of the time, Pallas kernels for 47%

profile of v4, /device:TPU:13, one launch (start us, length us, event | category | flops | bytes accessed | tf_op | source)
XLA Modules:
  0.0 107.2 jit_solution(14465888024073126152)
XLA Ops:
  6.5 1.2 %copy-done.1 = f32[16,32,512]{2,1,0:T(8,128)S(1)} copy-done((f32[16,32,512]{2,1,0:T(8,128)S(1)}, f32[16,32,512]{2,1,0:T(8,128)}, u32[]{:S(2)}) %copy-start.1) | copy-done | bytes 1048600
  7.8 1.1 %copy-done.4 = bf16[640,512]{1,0:T(8,128)(2,1)S(1)} copy-done((bf16[640,512]{1,0:T(8,128)(2,1)S(1)}, bf16[640,512]{1,0:T(8,128)(2,1)}, u32[]{:S(2)}) %copy-start.4) | copy-done | bytes 655384
  8.9 1.1 %copy-done.6 = bf16[640,512]{1,0:T(8,128)(2,1)S(1)} copy-done((bf16[640,512]{1,0:T(8,128)(2,1)S(1)}, bf16[640,512]{1,0:T(8,128)(2,1)}, u32[]{:S(2)}) %copy-start.6) | copy-done | bytes 655384
  9.9 1.6 %copy-done.8 = bf16[16,4,32,512]{3,2,1,0:T(8,128)(2,1)S(1)} copy-done((bf16[16,4,32,512]{3,2,1,0:T(8,128)(2,1)S(1)}, bf16[16,4,32,512]{3,2,1,0:T(8,128)(2,1)}, u32[]{:S(2)}) %copy-start.8) | copy-done | bytes 2097176
  11.5 0.7 copy-done.13
  12.2 9.3 %shard_map.118 = (f32[16,32,512]{2,1,0:T(8,128)S(1)}, bf16[16,32,640]{2,1,0:T(8,128)(2,1)}, bf16[16,32,512]{2,1,0:T(8,128)(2,1)S(1)}) custom-call(f32[4]{0:T(128)S(1)} %copy-done.13, f32[16,32,512]{2,1,0:T(8,128)S(1)} %copy-done.1, bf16[16,4,32,512]{3,2,1,0:T(8,128)(2,1)S(1)} %copy-done.8, bf16[640,512]{1,0:T(8,128)(2,1)S(1)} %copy-done.4, ...), custom_call_target="tpu_custom_call" | custom-call | tf_op jit(solution)/shard_map/pallas_call | solution.py:391
  21.5 1.0 copy-done.9
  22.5 16.7 %shard_map.119 = bf16[4,16,32,512]{3,2,1,0:T(8,128)(2,1)S(1)} custom-call(bf16[16,32,512]{2,1,0:T(8,128)(2,1)S(1)} %get-tuple-element.10.x_ref), custom_call_target="tpu_custom_call" | custom-call | tf_op jit(solution)/shard_map/pallas_call | solution.py:352
  39.2 1.1 %constant_dynamic-slice_fusion.kron_ref = bf16[256,1024]{1,0:T(8,128)(2,1)S(1)} fusion(bf16[1024,1024]{1,0:T(8,128)(2,1)} %constant.7.clone, s32[]{:T(128)S(6)} %select_n.7), kind=kLoop, calls=%fused_computation.12 | loop fusion | bytes 1048580 | tf_op jit(solution)/shard_map/dynamic_slice | solution.py:381
  40.3 1.4 %copy-done.10 = f32[16,32,512]{2,1,0:T(8,128)S(1)} copy-done((f32[16,32,512]{2,1,0:T(8,128)S(1)}, f32[16,32,512]{2,1,0:T(8,128)}, u32[]{:S(2)}) %copy-start.10) | copy-done | bytes 1048600
  41.7 0.8 shard_map.120.x_ref
  42.5 9.7 %shard_map.121.field_ref = f32[8,4,16,128]{3,2,1,0:T(8,128)S(1)} custom-call(f32[4,16,128]{2,1,0:T(8,128)S(1)} %shard_map.120.x_ref), custom_call_target="tpu_custom_call" | custom-call | tf_op jit(solution)/shard_map/pallas_call | solution.py:352
  52.2 7.3 %shard_map.122.x_ref = f32[512,128]{1,0:T(8,128)S(1)} custom-call(s32[512]{0:T(512)S(1)} %bitcast.12, f32[8,4,16,128]{3,2,1,0:T(8,128)S(1)} %shard_map.121.field_ref, bf16[512,16,128]{2,1,0:T(8,128)(2,1)S(1)} %copy-done, s32[512,128]{1,0:T(8,128)S(1)} %copy-done.11), custom_call_target="tpu_custom_call" | custom-call | tf_op jit(solution)/shard_map/pallas_call | solution.py:340
  59.6 10.7 %shard_map.123.ev_ref = f32[512,128]{1,0:T(8,128)S(1)} custom-call(f32[512,128]{1,0:T(8,128)S(1)} %shard_map.122.x_ref), custom_call_target="tpu_custom_call" | custom-call | tf_op jit(solution)/shard_map/pallas_call | solution.py:352
  70.3 0.1 convert_select_fusion.w_ref
  70.4 6.6 %shard_map.124 = f32[8,128,64]{2,1,0:T(8,128)S(1)} custom-call(s32[512]{0:T(512)S(1)} %bitcast.13, bf16[512,16,128]{2,1,0:T(8,128)(2,1)S(1)} %copy-done, s32[512,128]{1,0:T(8,128)S(1)} %copy-done.11, f32[512,128]{1,0:T(8,128)S(1)} %shard_map.123.ev_ref, f32[512,128]{1,0:T(8,128)S(1)} %convert_element_type.6.inn_ref, f32[512,128]{1,0:T(8,128)S(1)} %convert_select_fusion.w_ref), custom_call_target="tpu_custom_call" | custom-call | tf_op jit(solution)/shard_map/pallas_call | solution.py:340
  77.0 0.9 copy.16
  77.9 1.0 copy.20
  78.9 0.1 pad.5.clone
  79.0 0.1 fusion.3
  79.1 0.1 fusion.x_ref
  79.1 15.1 %shard_map.125 = f32[4,16,640]{2,1,0:T(8,128)S(1)} custom-call(f32[8,16,640]{2,1,0:T(8,128)S(1)} %fusion.x_ref), custom_call_target="tpu_custom_call" | custom-call | tf_op jit(solution)/shard_map/pallas_call | solution.py:352
  94.3 1.7 %copy-done.3 = bf16[64,32,640]{2,1,0:T(8,128)(2,1)S(1)} copy-done((bf16[64,32,640]{2,1,0:T(8,128)(2,1)S(1)}, bf16[64,32,640]{2,1,0:T(8,128)(2,1)}, u32[]{:S(2)}) %copy-start.3) | copy-done | bytes 2621464
  96.0 4.3 %shard_map.126 = f32[16,32,512]{2,1,0:T(8,128)} custom-call(bf16[64,32,640]{2,1,0:T(8,128)(2,1)S(1)} %copy-done.3, f32[64,640]{1,0:T(8,128)S(1)} %bitcast.11, bf16[256,1024]{1,0:T(8,128)(2,1)S(1)} %constant_dynamic-slice_fusion.kron_ref, bf16[640,512]{1,0:T(8,128)(2,1)S(1)} %copy-done.5, bf16[640,512]{1,0:T(8,128)(2,1)S(1)} %copy-done.7, ...), custom_call_target="tpu_custom_call" | custom-call | tf_op jit(solution)/shard_map/pallas_call | solution.py:340
  (31 shorter events, 0.1 us)
Async XLA Ops:
  6.5 87.7 %all-gather.2.cloned.1.call-start = ((), (), s32[]{:S(2)}) async-start(), calls=%async_computation | async-start | bytes 3276800 | tf_op jit(solution)/shard_map/all_gather | solution.py:415
  6.5 1.2 %copy-start.1 = (f32[16,32,512]{2,1,0:T(8,128)S(1)}, f32[16,32,512]{2,1,0:T(8,128)}, u32[]{:S(2)}) copy-start(f32[16,32,512]{2,1,0:T(8,128)} %control_ref.3) | copy-start | bytes 3145732
  7.8 1.1 %copy-start.4 = (bf16[640,512]{1,0:T(8,128)(2,1)S(1)}, bf16[640,512]{1,0:T(8,128)(2,1)}, u32[]{:S(2)}) copy-start(bf16[640,512]{1,0:T(8,128)(2,1)} %constant.22.clone.hi_ref) | copy-start | bytes 1966084
  8.9 1.1 %copy-start.6 = (bf16[640,512]{1,0:T(8,128)(2,1)S(1)}, bf16[640,512]{1,0:T(8,128)(2,1)}, u32[]{:S(2)}) copy-start(bf16[640,512]{1,0:T(8,128)(2,1)} %constant.23.clone.lo_ref) | copy-start | bytes 1966084
  9.9 1.6 %copy-start.8 = (bf16[16,4,32,512]{3,2,1,0:T(8,128)(2,1)S(1)}, bf16[16,4,32,512]{3,2,1,0:T(8,128)(2,1)}, u32[]{:S(2)}) copy-start(bf16[16,4,32,512]{3,2,1,0:T(8,128)(2,1)} %members_ref.1) | copy-start | bytes 6291460
  11.5 0.7 copy-start.13
  21.5 1.0 copy-start.9
  40.3 11.9 %copy-start = (bf16[512,16,128]{2,1,0:T(8,128)(2,1)S(1)}, bf16[512,16,128]{2,1,0:T(8,128)(2,1)}, u32[]{:S(2)}) copy-start(bf16[512,16,128]{2,1,0:T(8,128)(2,1)} %kern_ref.3) | copy-start | bytes 6291460
  40.3 1.4 %copy-start.10 = (f32[16,32,512]{2,1,0:T(8,128)S(1)}, f32[16,32,512]{2,1,0:T(8,128)}, u32[]{:S(2)}) copy-start(f32[16,32,512]{2,1,0:T(8,128)} %copy-done.9) | copy-start | bytes 3145732
  41.7 10.5 %copy-start.11 = (s32[512,128]{1,0:T(8,128)S(1)}, s32[512,128]{1,0:T(8,128)}, u32[]{:S(2)}) copy-start(s32[512,128]{1,0:T(8,128)} %col_ref.3) | copy-start | bytes 786436
  41.7 10.5 %copy-start.12 = (s32[512,1]{0,1:T(1,128)S(1)}, s32[512,1]{0,1:T(1,128)}, u32[]{:S(2)}) copy-start(s32[512,1]{0,1:T(1,128)} %param.18) | copy-start | bytes 6148
  42.4 27.8 %copy-start.14 = (bf16[512,128]{1,0:T(8,128)(2,1)S(1)}, bf16[512,128]{1,0:T(8,128)(2,1)}, u32[]{:S(2)}) copy-start(bf16[512,128]{1,0:T(8,128)(2,1)} %param.16) | copy-start | bytes 393220
  42.5 27.8 %copy-start.15 = (bf16[512,128]{1,0:T(8,128)(2,1)S(1)}, bf16[512,128]{1,0:T(8,128)(2,1)}, u32[]{:S(2)}) copy-start(bf16[512,128]{1,0:T(8,128)(2,1)} %param.17) | copy-start | bytes 393220
  42.5 27.8 %copy-start.16 = (s32[512]{0:T(512)S(1)}, s32[512]{0:T(512)}, u32[]{:S(2)}) copy-start(s32[512]{0:T(512)} %param.20) | copy-start | bytes 6148
  77.0 17.3 %copy-start.2 = (f32[16,32,512]{2,1,0:T(8,128)S(1)}, f32[16,32,512]{2,1,0:T(8,128)}, u32[]{:S(2)}) copy-start(f32[16,32,512]{2,1,0:T(8,128)} %control_ref.3) | copy-start | bytes 3145732
  77.0 17.3 %copy-start.5 = (bf16[640,512]{1,0:T(8,128)(2,1)S(1)}, bf16[640,512]{1,0:T(8,128)(2,1)}, u32[]{:S(2)}) copy-start(bf16[640,512]{1,0:T(8,128)(2,1)} %constant.22.clone.hi_ref) | copy-start | bytes 1966084
  77.0 17.3 %copy-start.7 = (bf16[640,512]{1,0:T(8,128)(2,1)S(1)}, bf16[640,512]{1,0:T(8,128)(2,1)}, u32[]{:S(2)}) copy-start(bf16[640,512]{1,0:T(8,128)(2,1)} %constant.23.clone.lo_ref) | copy-start | bytes 1966084
  94.3 1.7 %copy-start.3 = (bf16[64,32,640]{2,1,0:T(8,128)(2,1)S(1)}, bf16[64,32,640]{2,1,0:T(8,128)(2,1)}, u32[]{:S(2)}) copy-start(bf16[64,32,640]{2,1,0:T(8,128)(2,1)} %all-gather.2.cloned.1.call-done.mixed_ref) | copy-start | bytes 7864324
Sparse Core Ops, SparseCore 0:
  39.3 25.6 all-gather.1
